TPU v7x, 128 devices: a whole 4x4x4 slice. The times are simulated.
128 devices in a mesh: lon: 16 (over z, x_lo, core), ens: 8 (over y, x_hi).
Axes of the slice: x: 4 (x_hi: 2, x_lo: 2; x = x_hi * 2 + x_lo), y: 4, z: 4, core: 2. Of those that a mesh axis runs over, the one named last changes fastest.
Arguments:
- features: bfloat16 [16, 4, 1440, 512], P('ens', None, 'lon'), may hold values from -6 to 6
- weight: bfloat16 [2048, 512], P('ens'), may hold values from -0.125 to 0.125
- grad_out: bfloat16 [16, 4, 1440, 512], P('ens', None, 'lon'), may hold values from -6 to 6
- band_width: int32 [4], replicated, may hold values from 4 to 1440, as said below
- band_start: int32 [4], replicated, may hold values from -722 to 0, as said below
Outputs:
- output: bfloat16 [16, 4, 1440, 512], P('ens', None, 'lon')
- grad_input: bfloat16 [16, 4, 1440, 512], P('ens', None, 'lon')
- grad_weight: float32 [2048, 512], P('ens')
Inputs may be any that keep to these rules, and one draw needn't show every extreme that they name: band_width[0] equals 1440, so the first row's support covers the whole circle; the last row's width is 4. The support of row l is the band_width[l] consecutive longitudes starting band_start[l] cells from the target, taken cyclically; the first row starts at -720 - 2 and the last row at 0.
All inputs are finite; a program needn't handle non-finite values.
Results may differ from a plain program's by a relative error of at most 0.0055.
Values may be sent and summed in bfloat16 or wider, within the bound.
A program may use at most 128 MiB of HBM per device.

v0:
```python
import jax
import jax.numpy as jnp
from jax import lax
from jax.sharding import PartitionSpec as P

K = 4


def make_basis(widths, starts, targets, sources, circle):
    relative = jnp.mod(
        sources[None, None, :] - targets[None, :, None] - starts[:, None, None], circle
    )
    inside = relative < widths[:, None, None]
    width_float = widths.astype(jnp.float32)[:, None, None]
    position = (relative.astype(jnp.float32) + 0.5) * (K - 1) / width_float
    orders = jnp.arange(K).astype(jnp.float32)
    hats = jnp.maximum(0.0, 1.0 - jnp.abs(position[:, None] - orders[None, :, None, None]))
    hats = hats / jnp.sqrt(width_float)[:, None]
    return jnp.where(inside[:, None], hats, 0.0).astype(jnp.bfloat16)


def on_device(features, weight, grad_out, band_width, band_start):
    members, latitudes, lon_count, channels = features.shape
    circle = lon_count * lax.axis_size("lon")
    own_targets = lax.axis_index("lon") * lon_count + jnp.arange(lon_count)
    piece = lax.all_gather(features, "lon", axis=2, tiled=True)
    sources = jnp.arange(piece.shape[2])
    kernel = make_basis(band_width, band_start, own_targets, sources, circle)
    response = jnp.einsum("lkts,mlsc->mltkc", kernel, piece, preferred_element_type=jnp.float32)
    piece = lax.all_gather(grad_out, "lon", axis=2, tiled=True)
    targets = jnp.arange(piece.shape[2])
    kernel = make_basis(band_width, band_start, targets, own_targets, circle)
    adjoint = jnp.einsum("lkts,mltd->mlskd", kernel, piece, preferred_element_type=jnp.float32)
    row_count = members * latitudes * lon_count
    response = response.astype(jnp.bfloat16).reshape(row_count, K * channels)
    adjoint = adjoint.astype(jnp.bfloat16).reshape(row_count, K, channels)
    full_weight = lax.all_gather(weight, "ens", axis=0, tiled=True)
    output = jnp.dot(response, full_weight, preferred_element_type=jnp.float32).astype(jnp.bfloat16)
    grad_input = jnp.einsum(
        "rkd,kcd->rc",
        adjoint,
        full_weight.reshape(K, channels, channels),
        preferred_element_type=jnp.float32,
    ).astype(jnp.bfloat16)
    local_grad = lax.dot_general(
        response,
        grad_out.reshape(row_count, channels),
        (((0,), (0,)), ((), ())),
        preferred_element_type=jnp.float32,
    )
    summed = lax.psum(local_grad, "lon")
    grad_weight = lax.psum_scatter(summed, "ens", scatter_dimension=0, tiled=True)
    return (output.reshape(features.shape), grad_input.reshape(features.shape), grad_weight)


def solution(mesh):
    placed = (P("ens", None, "lon", None), P("ens", None), P("ens", None, "lon", None), P(), P())
    return jax.shard_map(
        on_device,
        mesh=mesh,
        in_specs=placed,
        out_specs=(P("ens", None, "lon", None), P("ens", None, "lon", None), P("ens", None)),
        check_vma=False,
    )
```

profile of v0, /device:TPU:1, one launch (start us, length us, event | category | flops | bytes accessed | tf_op | source)
XLA Modules:
  0.0 424.3 jit_solution(13489745119735881193)
XLA Ops:
  7.2 0.0 copy-start.1
  7.2 0.0 all-gather.4.cloned.1.call-start
  7.2 2.3 copy.20
  9.5 0.0 copy-start.3
  9.5 0.0 all-gather.4.cloned.1.call-update
  9.5 0.0 all-gather.8.cloned.1.call-start
  9.6 0.0 copy-done.1
  9.6 1.1 copy.23
  10.7 0.0 copy-start.2
  10.7 0.0 all-gather.8.cloned.1.call-update
  10.7 0.0 reduce-scatter.2.cloned.1.call-start
  10.8 0.1 copy.27
  11.0 0.0 copy-done.3
  11.0 0.2 reshape.118
  11.2 0.1 iota_subtract_fusion.1
  11.3 0.0 copy-done.2
  11.4 2.6 fusion.27
  14.0 1.8 multiply_divide_fusion.1
  15.8 66.3 %all-gather.4.cloned.1.call-done = bf16[2,4,1440,512]{3,1,0,2:T(4,128)(2,1)} async-done(((bf16[2,4,90,512]{3,1,0,2:T(4,128)(2,1)}), bf16[2,4,1440,512]{3,1,0,2:T(4,128)(2,1)}) %all-gather.4.cloned.1.call-update) | async-done | bytes 11796496 | tf_op jit(solution)/shard_map/all_gather | solution.py:26
  82.2 14.0 %convert_bitcast_fusion.1 = bf16[2,4,90,4,512]{4,2,0,3,1:T(8,128)(2,1)S(1)} fusion(bf16[2,4,1440,512,1]{3,1,0,2,4:T(4,128)(2,1)} %bitcast.37, f32[4]{0:T(128)S(1)} %convert_sqrt_fusion, f32[4]{0:T(128)S(1)} %iota_convert_fusion, f32[4,90,1440]{2,1,0:T(8,128)S(1)} %multiply_divide_fusion.1, pred[4,90,1440]{2,1,0:T(8,128)(4,1)} %fusion.27), kind=kOutput, calls=%fused_computation.23 | convolution fusion | flops 4262722560 | bytes 17337632 | tf_op jit(solution)/shard_map/lkts,mlsc->mltkc/dot_general | solution.py:29
  96.2 2.5 copy.22
  98.7 0.9 copy.38
  99.6 0.0 copy-start
  99.6 1.6 copy-done
  101.2 3.8 fusion.44
  105.0 0.0 reduce-scatter.2.cloned.1.call-update
  105.1 0.0 all-gather.6.cloned.1.call-start
  105.1 0.5 all-gather.6.cloned.1.call-update
  105.7 0.0 all-reduce.2.cloned.1.call-start
  105.7 0.1 iota_subtract_fusion
  105.8 3.0 multiply_divide_fusion
  108.8 2.6 fusion.24
  111.4 42.2 %all-gather.8.cloned.1.call-done = bf16[2,4,1440,512]{3,1,0,2:T(4,128)(2,1)} async-done(((bf16[2,4,90,512]{3,1,0,2:T(4,128)(2,1)}), bf16[2,4,1440,512]{3,1,0,2:T(4,128)(2,1)}) %all-gather.8.cloned.1.call-update) | async-done | bytes 11796496 | tf_op jit(solution)/shard_map/all_gather | solution.py:30
  153.6 14.7 %convert_bitcast_fusion = bf16[2,4,90,4,512]{4,2,0,3,1:T(8,128)(2,1)S(1)} fusion(bf16[2,4,1440,512,1]{3,1,0,2,4:T(4,128)(2,1)} %bitcast.36, f32[4]{0:T(128)S(1)} %convert_sqrt_fusion, f32[4]{0:T(128)S(1)} %iota_convert_fusion, f32[4,1440,90]{1,2,0:T(8,128)} %multiply_divide_fusion, pred[4,1440,90]{1,2,0:T(8,128)(4,1)} %fusion.24), kind=kOutput, calls=%fused_computation.22 | convolution fusion | flops 4262722560 | bytes 17337632 | tf_op jit(solution)/shard_map/lkts,mltd->mlskd/dot_general | solution.py:33
  168.4 73.1 %reduce-scatter.2.cloned.1.call-done = f32[256,512]{1,0:T(8,128)} async-done(((f32[2048,512]{1,0:T(8,128)}), f32[256,512]{1,0:T(8,128)}) %reduce-scatter.2.cloned.1.call-update) | async-done | bytes 524304 | tf_op jit(solution)/shard_map/reduce_scatter | solution.py:52
  241.5 0.0 all-reduce.2.cloned.1.call-update
  241.5 55.8 %all-gather.6.cloned.1.call-done = bf16[2048,512]{1,0:T(8,128)(2,1)} async-done(((bf16[256,512]{1,0:T(8,128)(2,1)}), bf16[2048,512]{1,0:T(8,128)(2,1)}) %all-gather.6.cloned.1.call-update) | async-done | bytes 2097168 | tf_op jit(solution)/shard_map/all_gather | solution.py:37
  297.3 5.0 %convolution_convert_fusion = bf16[720,512]{1,0:T(8,128)(2,1)} fusion(bf16[720,2048]{1,0:T(8,128)(2,1)} %bitcast.34, bf16[2048,512]{1,0:T(8,128)(2,1)} %all-gather.6.cloned.1.call-done), kind=kOutput, calls=%fused_computation.39 | convolution fusion | flops 1510318080 | bytes 5783552 | tf_op jit(solution)/shard_map/dot_general | solution.py:38
  302.3 2.2 reshape.114
  304.5 2.6 copy.28
  307.1 0.0 copy-start.4
  307.1 2.5 copy.25
  309.6 0.0 copy-done.4
  309.6 1.7 bitcast_convert_fusion
  311.4 0.2 reshape.117
  311.6 1.4 copy.29
  313.0 103.0 %all-reduce.2.cloned.1.call-done = f32[256,512]{1,0:T(8,128)} async-done(((f32[256,512]{1,0:T(8,128)}), f32[256,512]{1,0:T(8,128)}) %all-reduce.2.cloned.1.call-update) | async-done | bytes 524304 | tf_op jit(solution)/shard_map/psum | solution.py:51
  416.0 1.9 copy.52
  (4 shorter events, 0.0 us)
Async XLA Ops:
  7.2 2.4 copy-start.1
  7.2 75.0 %all-gather.4.cloned.1.call-start = ((), (), s32[]{:S(2)}) async-start(), calls=%async_computation.1 | async-start | bytes 12533760 | tf_op jit(solution)/shard_map/all_gather | solution.py:26
  9.5 1.4 copy-start.3
  9.5 144.1 %all-gather.8.cloned.1.call-start = ((), (), s32[]{:S(2)}) async-start(), calls=%async_computation.3 | async-start | bytes 12533760 | tf_op jit(solution)/shard_map/all_gather | solution.py:30
  10.7 0.7 copy-start.2
  10.7 230.7 %reduce-scatter.2.cloned.1.call-start = ((), (), s32[]{:S(2)}) async-start(), calls=%async_computation.4 | async-start | bytes 4718592 | tf_op jit(solution)/shard_map/reduce_scatter | solution.py:52
  99.6 1.6 copy-start
  105.1 192.2 %all-gather.6.cloned.1.call-start = ((), (), s32[]{:S(2)}) async-start(), calls=%async_computation.2 | async-start | bytes 2359296 | tf_op jit(solution)/shard_map/all_gather | solution.py:37
  105.7 310.3 %all-reduce.2.cloned.1.call-start = ((), (), s32[]{:S(2)}) async-start(), calls=%async_computation.5 | async-start | bytes 1048576 | tf_op jit(solution)/shard_map/psum | solution.py:51
  307.1 2.5 copy-start.4
Sparse Core Ops, SparseCore 0:
  10.3 71.8 all-gather.3
  84.4 69.1 all-gather.7
  157.5 83.9 reduce-scatter.1
  244.0 53.2 all-gather.5
  299.8 116.1 all-reduce.1
where the time goes:
time: 425 us; the launch traced here: 424 us
  waiting for transfers between devices  341 us (80%)
  matrix products  39.4 us (9%)
  local copies, waits for them, and re-layouts  19.6 us (5%)
  between operations  13.9 us (3%)
  other arithmetic  10.3 us (2%)
    psum x1, waiting for transfers between devices, on_device(): summed = lax.psum(local_grad, 'lon')  103 us
    reduce_scatter x1, waiting for transfers between devices, on_device(): lax.psum_scatter(summed, 'ens', scatter_dimension=0, tiled=True)  73.1 us
    all_gather x1, waiting for transfers between devices, on_device(): piece = lax.all_gather(features, 'lon', axis=2, tiled=True)  66.3 us
    all_gather x1, waiting for transfers between devices, on_device(): full_weight = lax.all_gather(weight, 'ens', axis=0, tiled=True)  55.8 us
    all_gather x1, waiting for transfers between devices, on_device(): piece = lax.all_gather(grad_out, 'lon', axis=2, tiled=True)  42.2 us
    dot_general x1, matrix products, on_device(): jnp.einsum('lkts,mltd->mlskd', kernel, piece, preferred_element_type=jnp....  14.7 us
    dot_general x1, matrix products, on_device(): jnp.einsum('lkts,mlsc->mltkc', kernel, piece, preferred_element_type=jnp....  14 us
    unnamed x17, local copies, waits for them, and re-layouts  12 us
  transfers between devices with their start and end apart: 5, of which 5 were waited for; matrix products, arithmetic and copies ran while one was open for 15% of the time, Pallas kernels for 0%

commit v1 on v0

v1 whole, which is shorter than its diff:
```python
import functools

import jax
import jax.numpy as jnp
from jax import lax
from jax.experimental import pallas as pl
from jax.experimental.pallas import tpu as pltpu
from jax.sharding import PartitionSpec as P

K = 4
BF = jnp.bfloat16
F32 = jnp.float32


def remote(src, dst, send, recv, lon, ens):
    return pltpu.make_async_remote_copy(
        src_ref=src,
        dst_ref=dst,
        send_sem=send,
        recv_sem=recv,
        device_id={"lon": lon, "ens": ens},
        device_id_type=pl.DeviceIdType.MESH,
    )


def fill_strip(strip, width, start, block, padded, count, flip):
    circle = block * count
    step = min(128, padded * count)
    row = lax.broadcasted_iota(jnp.int32, (padded, step), 0)
    lane = lax.broadcasted_iota(jnp.int32, (padded, step), 1)
    wide = jnp.full((1, step), width.astype(F32), F32)
    scale = 1.0 / jnp.sqrt(wide)
    for first in range(0, padded * count, step):
        column = lane + first
        low = first // padded
        part = jnp.full_like(column, low)
        for edge in range(low + 1, (first + step - 1) // padded + 1):
            part = part + (column >= edge * padded).astype(jnp.int32)
        inner = column - part * padded
        place = inner + part * block
        valid = (inner < block) & (row < block)
        away = (row - place if flip else place - row) - start
        away = jnp.where(away < 0, away + circle, away)
        away = jnp.where(away >= circle, away - circle, away)
        inside = valid & (away < width)
        position = (away.astype(F32) + 0.5) * (K - 1) / wide
        for k in range(K):
            hat = jnp.maximum(0.0, 1.0 - jnp.abs(position - float(k))) * scale
            strip[pl.ds(k * padded, padded), pl.ds(first, step)] = jnp.where(inside, hat, 0.0).astype(BF)


def kernel(
    count, groups,
    f_ref, g_ref, w_ref, width_ref, start_ref,
    out_ref, gi_ref, gw_ref,
    f_send, g_send, f_ext, g_ext, f_strip, g_strip, resp, adj, w_all,
    out_own, gi_own, out_in, gi_in,
    gw_own, gw_half, gw_mate, gw_sum, gw_ens, gw_lon, gw_lon_in, gw_full,
    f_ss, f_rs, f_fs, g_ss, g_rs, g_fs, w_ss, w_rs, w_ms, w_mr,
    out_ss, out_rs, gi_ss, gi_rs,
    a_ss, a_rs, b_ss, b_rs, c_ss, c_rs, d_ss, d_rs,
):
    members, rows, block, channels = f_ref.shape
    padded = f_send.shape[1]
    tasks = members * rows
    lon = lax.axis_index("lon")
    ens = lax.axis_index("ens")
    half = lax.rem(lon, 2)
    task = lax.div(lon, 2)
    mate = lon + 1 - 2 * half

    barrier = pltpu.get_barrier_semaphore()

    @pl.loop(1, count)
    def _(o):
        pl.semaphore_signal(barrier, inc=1, device_id={"lon": lax.rem(lon + o, count), "ens": ens},
                            device_id_type=pl.DeviceIdType.MESH)

    @pl.loop(1, groups)
    def _(o):
        pl.semaphore_signal(barrier, inc=1, device_id={"lon": lon, "ens": lax.rem(ens + o, groups)},
                            device_id_type=pl.DeviceIdType.MESH)

    def stage(ref, buffer, ext):
        for q in range(tasks):
            buffer[q, pl.ds(padded - 16, 16), :] = jnp.zeros((16, channels), BF)
            buffer[q, pl.ds(0, block), :] = ref[q // rows, q % rows]
        ext[lon] = buffer[task]

    piece = w_ref.shape[0] // 2
    w_all[ens, 0] = w_ref[0:piece]
    w_all[ens, 1] = w_ref[piece:]
    stage(g_ref, g_send, g_ext)
    stage(f_ref, f_send, f_ext)

    pl.semaphore_wait(barrier, count - 1 + groups - 1)

    def w_copy(o):
        return remote(w_all.at[ens, half], w_all.at[ens, half], w_ss.at[o], w_rs.at[ens],
                      lon, lax.rem(ens + o, groups))

    def w_from(o):
        other = lax.rem(ens + groups - o, groups)
        return remote(w_all.at[other, half], w_all.at[other, half], w_ss.at[o], w_rs.at[other], lon, other)

    def in_copy(buffer, ext, ss, rs, o):
        q = lax.rem(task + o, tasks)
        return remote(buffer.at[q], ext.at[lon], ss.at[o], rs.at[lon], 2 * q + half, ens)

    def in_from(ext, ss, rs, o):
        slot = 2 * lax.rem(task + tasks - o, tasks) + half
        return remote(ext.at[slot], ext.at[slot], ss.at[o], rs.at[slot], slot, ens)

    def forward(ext, fs, rs, o):
        slot = 2 * lax.rem(task + tasks - o, tasks) + half
        return remote(ext.at[slot], ext.at[slot], fs.at[o], rs.at[slot], mate, ens)

    def forwarded(ext, fs, rs, o):
        slot = 2 * lax.rem(task + tasks - o, tasks) + 1 - half
        return remote(ext.at[slot], ext.at[slot], fs.at[o], rs.at[slot], mate, ens)

    @pl.loop(1, groups)
    def _(o):
        w_copy(o).start()

    @pl.loop(1, tasks)
    def _(o):
        in_copy(g_send, g_ext, g_ss, g_rs, o).start()

    @pl.loop(1, tasks)
    def _(o):
        in_copy(f_send, f_ext, f_ss, f_rs, o).start()

    forward(g_ext, g_fs, g_rs, 0).start()
    forward(f_ext, f_fs, f_rs, 0).start()

    row = lax.rem(task, rows)
    fill_strip(g_strip, width_ref[row], start_ref[row], block, padded, count, True)
    fill_strip(f_strip, width_ref[row], start_ref[row], block, padded, count, False)

    def arrive(ext, ss, fs, rs):
        @pl.loop(1, tasks)
        def _(o):
            in_from(ext, ss, rs, o).wait_recv()
            forward(ext, fs, rs, o).start()

        @pl.loop(0, tasks)
        def _(o):
            forwarded(ext, fs, rs, o).wait_recv()

        @pl.loop(0, count - 1)
        def _(b):
            ext[count + b] = ext[b]

    def convolve(strip, ext, result):
        @pl.loop(0, tasks)
        def _(n):
            window = ext[pl.ds(2 * n + half, count)].reshape(count * padded, channels)
            total = jnp.dot(strip[...], window, preferred_element_type=F32)
            for k in range(K):
                result[k, n] = total[k * padded:(k + 1) * padded].astype(BF)

    per = groups // K

    def weight_of(k):
        return w_all[pl.ds(k * per, per)].reshape(channels, channels)

    def back_copy(own, into, ss, rs, n):
        return remote(own.at[n], into.at[task], ss.at[n], rs.at[task], 2 * n + half, ens)

    def back_from(own, into, ss, rs, n):
        return remote(own.at[n], into.at[n], ss.at[n], rs.at[n], 2 * n + half, ens)

    def mix(source, own, into, ss, rs, flip):
        chunk = tasks // 2
        for c in range(2):
            total = None
            for k in range(K):
                part = source[k, pl.ds(c * chunk, chunk)].reshape(chunk * padded, channels)
                dims = (((1,), (1 if flip else 0,)), ((), ()))
                term = lax.dot_general(part, weight_of(k), dims, preferred_element_type=F32)
                total = term if total is None else total + term
            own[pl.ds(c * chunk, chunk)] = total.astype(BF).reshape(chunk, padded, channels)
            for n in range(c * chunk, (c + 1) * chunk):
                @pl.when(n != task)
                def _():
                    back_copy(own, into, ss, rs, n).start()

    arrive(g_ext, g_ss, g_fs, g_rs)

    @pl.loop(1, groups)
    def _(o):
        w_from(o).wait_recv()

    w_mate = remote(w_all.at[:, half], w_all.at[:, half], w_ms, w_mr, mate, ens)
    w_mate.start()
    convolve(g_strip, g_ext, adj)
    remote(w_all.at[:, 1 - half], w_all.at[:, 1 - half], w_ms, w_mr, mate, ens).wait_recv()
    mix(adj, gi_own, gi_in, gi_ss, gi_rs, True)

    arrive(f_ext, f_ss, f_fs, f_rs)
    own_rows = jnp.concatenate([f_ext[2 * n + half] for n in range(tasks)], axis=0)
    turned = own_rows.T
    for k in range(K):
        term = jnp.dot(turned, adj[k].reshape(tasks * padded, channels), preferred_element_type=F32)
        gw_own[pl.ds(k * per, per)] = term.reshape(per, 2, piece, channels)
    gw_half[...] = gw_own[:, 1 - half].astype(BF)
    a_copy = remote(gw_half, gw_mate, a_ss, a_rs, mate, ens)
    a_copy.start()

    convolve(f_strip, f_ext, resp)

    a_copy.wait_recv()
    gw_sum[...] = (gw_own[:, half] + gw_mate[...].astype(F32)).astype(BF)

    def b_copy(o):
        other = lax.rem(ens + o, groups)
        return remote(gw_sum.at[other], gw_ens.at[ens], b_ss.at[o], b_rs.at[ens], lon, other)

    def b_from(o):
        other = lax.rem(ens + groups - o, groups)
        return remote(gw_sum.at[other], gw_ens.at[other], b_ss.at[o], b_rs.at[other], lon, other)

    @pl.loop(1, groups)
    def _(o):
        b_copy(o).start()

    gw_ens[ens] = gw_sum[ens]
    mix(resp, out_own, out_in, out_ss, out_rs, False)

    @pl.loop(1, groups)
    def _(o):
        b_from(o).wait_recv()

    total = gw_ens[0].astype(F32)
    for e in range(1, groups):
        total = total + gw_ens[e].astype(F32)
    gw_lon[...] = total.astype(BF).reshape(gw_lon.shape)

    def c_copy(o):
        q = lax.rem(task + o, tasks)
        return remote(gw_lon.at[q], gw_lon_in.at[task], c_ss.at[o], c_rs.at[task], 2 * q + half, ens)

    def c_from(o):
        q = lax.rem(task + tasks - o, tasks)
        return remote(gw_lon.at[q], gw_lon_in.at[q], c_ss.at[o], c_rs.at[q], 2 * q + half, ens)

    @pl.loop(1, tasks)
    def _(o):
        c_copy(o).start()

    gw_lon_in[task] = gw_lon[task]

    @pl.loop(1, tasks)
    def _(o):
        c_from(o).wait_recv()

    total = gw_lon_in[0].astype(F32)
    for q in range(1, tasks):
        total = total + gw_lon_in[q].astype(F32)
    gw_full[lon] = total

    def d_copy(o):
        return remote(gw_full.at[lon], gw_full.at[lon], d_ss.at[o], d_rs.at[lon], lax.rem(lon + o, count), ens)

    def d_from(o):
        other = lax.rem(lon + count - o, count)
        return remote(gw_full.at[other], gw_full.at[other], d_ss.at[o], d_rs.at[other], other, ens)

    @pl.loop(1, count)
    def _(o):
        d_copy(o).start()

    def finish(ref, own, into, ss, rs):
        into[task] = own[task]
        for q in range(tasks):
            @pl.when(q != task)
            def _():
                back_from(own, into, ss, rs, q).wait_recv()
            ref[q // rows, q % rows] = into[q, pl.ds(0, block), :]

    finish(gi_ref, gi_own, gi_in, gi_ss, gi_rs)
    finish(out_ref, out_own, out_in, out_ss, out_rs)

    @pl.loop(1, count)
    def _(o):
        d_from(o).wait_recv()

    strip_rows = gw_full.shape[1]
    for q in range(tasks):
        for s in range(2):
            gw_ref[pl.ds(s * piece + q * strip_rows, strip_rows), :] = gw_full[2 * q + s]

    @pl.loop(1, groups)
    def _(o):
        w_copy(o).wait_send()
        b_copy(o).wait_send()

    w_mate.wait_send()
    a_copy.wait_send()

    @pl.loop(0, tasks)
    def _(o):
        forward(g_ext, g_fs, g_rs, o).wait_send()
        forward(f_ext, f_fs, f_rs, o).wait_send()

    @pl.loop(1, tasks)
    def _(o):
        in_copy(g_send, g_ext, g_ss, g_rs, o).wait_send()
        in_copy(f_send, f_ext, f_ss, f_rs, o).wait_send()
        c_copy(o).wait_send()

    @pl.loop(1, count)
    def _(o):
        d_copy(o).wait_send()

    for n in range(tasks):
        @pl.when(n != task)
        def _():
            back_copy(gi_own, gi_in, gi_ss, gi_rs, n).wait_send()
            back_copy(out_own, out_in, out_ss, out_rs, n).wait_send()


def on_device(features, weight, grad_out, band_width, band_start):
    members, rows, block, channels = features.shape
    count = lax.axis_size("lon")
    groups = lax.axis_size("ens")
    tasks = members * rows
    padded = -(-block // 16) * 16
    shard = weight.shape[0]
    piece = shard // 2
    strip_rows = piece // tasks
    vmem = pltpu.VMEM
    dma = pltpu.SemaphoreType.DMA
    field = vmem((tasks, padded, channels), BF)
    ext = vmem((2 * count, padded, channels), BF)
    strip = vmem((K * padded, count * padded), BF)
    wide = vmem((K, tasks, padded, channels), BF)
    scratch = [
        field, field, ext, ext, strip, strip, wide, wide,
        vmem((groups, 2, piece, channels), BF),
        field, field, field, field,
        vmem((groups, 2, piece, channels), F32),
        vmem((groups, piece, channels), BF),
        vmem((groups, piece, channels), BF),
        vmem((groups, piece, channels), BF),
        vmem((groups, piece, channels), BF),
        vmem((tasks, strip_rows, channels), BF),
        vmem((tasks, strip_rows, channels), BF),
        vmem((count, strip_rows, channels), F32),
        dma((tasks,)), dma((count,)), dma((tasks,)),
        dma((tasks,)), dma((count,)), dma((tasks,)),
        dma((groups,)), dma((groups,)), dma(()), dma(()),
        dma((tasks,)), dma((tasks,)), dma((tasks,)), dma((tasks,)),
        dma(()), dma(()), dma((groups,)), dma((groups,)),
        dma((tasks,)), dma((tasks,)), dma((count,)), dma((count,)),
    ]
    whole = pl.BlockSpec(memory_space=pltpu.VMEM)
    scalar = pl.BlockSpec(memory_space=pltpu.SMEM)
    return pl.pallas_call(
        functools.partial(kernel, count, groups),
        out_shape=(
            jax.ShapeDtypeStruct(features.shape, BF),
            jax.ShapeDtypeStruct(features.shape, BF),
            jax.ShapeDtypeStruct(weight.shape, F32),
        ),
        in_specs=[whole, whole, whole, scalar, scalar],
        out_specs=(whole, whole, whole),
        scratch_shapes=scratch,
        compiler_params=pltpu.CompilerParams(
            collective_id=0, has_side_effects=True, vmem_limit_bytes=60 * 1024 * 1024
        ),
    )(features, grad_out, weight, band_width, band_start)


def solution(mesh):
    placed = (P("ens", None, "lon", None), P("ens", None), P("ens", None, "lon", None), P(), P())
    return jax.shard_map(
        on_device,
        mesh=mesh,
        in_specs=placed,
        out_specs=(P("ens", None, "lon", None), P("ens", None, "lon", None), P("ens", None)),
        check_vma=False,
    )
```

time: 425 us -> 94.7 us (0.22)
  waiting for transfers between devices: 341 us -> 0 us
  Pallas kernels: 0 us -> 85.7 us
  matrix products: 39.4 us -> 0 us
  between operations: 13.9 us -> 0.66 us
  local copies, waits for them, and re-layouts: 19.6 us -> 8.12 us
  other arithmetic: 10.3 us -> 0 us
    all_gather x3 -> x0, waiting for transfers between devices: 164 us -> none  [the longest x1 66.3 us: on_device(): piece = lax.all_gather(features, 'lon', axis=2, tiled=True)]
    psum x1 -> x0, waiting for transfers between devices: 103 us -> none  [on_device(): summed = lax.psum(local_grad, 'lon')]
    pallas_call x0 -> x1, Pallas kernels: none -> 85.7 us  [on_device(): pl.pallas_call(functools.partial(kernel, count, groups), out_shape=(jax.S...]
    reduce_scatter x1 -> x0, waiting for transfers between devices: 73.1 us -> none  [on_device(): lax.psum_scatter(summed, 'ens', scatter_dimension=0, tiled=True)]
    dot_general x5 -> x0, matrix products: 39.4 us -> none  [the longest x1 14.7 us: on_device(): jnp.einsum('lkts,mltd->mlskd', kernel, piece, preferred_element_type=jnp....]
    unnamed x17 -> x9, local copies, waits for them, and re-layouts: 12 us -> 4.05 us
    lt x2 -> x0, other arithmetic: 5.24 us -> none  [make_basis(): inside = relative < widths[:, None, None]]
    convert_element_type x2 -> x0, local copies, waits for them, and re-layouts: 4.96 us -> none  [the longest x1 2.5 us: on_device(): adjoint = adjoint.astype(jnp.bfloat16).reshape(row_count, K, channels)]
  transfers between devices with their start and end apart: 5 -> 0, of which waited for: 5 -> 0; matrix products, arithmetic and copies ran while one was open for 15% -> 0% of each run, Pallas kernels for 0% -> 0%
where the time goes in v1:
time: 94.7 us; the launch traced here: 94.5 us
  Pallas kernels  85.7 us (90%)
  local copies, waits for them, and re-layouts  8.12 us (9%)
    pallas_call x1, Pallas kernels, on_device(): pl.pallas_call(functools.partial(kernel, count, groups), out_shape=(jax.S...  85.7 us
    pallas_call x2, local copies, waits for them, and re-layouts, on_device(): pl.pallas_call(functools.partial(kernel, count, groups), out_shape=(jax.S...  4.07 us
    unnamed x9, local copies, waits for them, and re-layouts  4.05 us

profile of v1, /device:TPU:1, one launch (start us, length us, event | category | flops | bytes accessed | tf_op | source)
XLA Modules:
  0.0 94.5 jit_solution(17341799408241047945)
XLA Ops:
  0.6 0.0 copy-start.1
  0.6 2.2 %copy.8.f_ref = bf16[2,4,90,512]{3,2,1,0:T(8,128)(2,1)} copy(bf16[2,4,90,512]{3,1,2,0:T(4,128)(2,1)} %param.5) | data formatting | bytes 1474560 | tf_op args[0]
  2.9 0.0 copy-done.1
  2.9 1.0 %copy.9.g_ref = bf16[2,4,90,512]{3,2,1,0:T(8,128)(2,1)} copy(bf16[2,4,90,512]{3,1,2,0:T(4,128)(2,1)S(1)} %copy-done.1) | data formatting | bytes 1474560 | tf_op args[2]
  3.9 85.7 %shard_map.76 = (bf16[2,4,90,512]{3,2,1,0:T(8,128)(2,1)}, bf16[2,4,90,512]{3,2,1,0:T(8,128)(2,1)}, f32[256,512]{1,0:T(8,128)}) custom-call(bf16[2,4,90,512]{3,2,1,0:T(8,128)(2,1)} %copy.8.f_ref, bf16[2,4,90,512]{3,2,1,0:T(8,128)(2,1)} %copy.9.g_ref, bf16[256,512]{1,0:T(8,128)(2,1)} %w_ref.1, s32[4]{0:T(128)} %width_ref.1, s32[4]{0:T(128)} %start_ref.1), custom_call_target="tpu_custom_call" | custom-call | tf_op jit(solution)/shard_map/pallas_call | solution.py:360
  89.6 0.0 copy-start
  89.6 2.6 %copy.10 = bf16[2,4,90,512]{3,1,2,0:T(4,128)(2,1)} copy(bf16[2,4,90,512]{3,2,1,0:T(8,128)(2,1)} %get-tuple-element.3) | data formatting | bytes 1474560 | tf_op jit(solution)/shard_map/pallas_call | solution.py:360
  92.3 0.0 copy-done
  92.3 0.0 copy-start.2
  92.3 1.4 %copy.11 = bf16[2,4,90,512]{3,1,2,0:T(4,128)(2,1)} copy(bf16[2,4,90,512]{3,2,1,0:T(8,128)(2,1)S(1)} %copy-done) | data formatting | bytes 1474560 | tf_op jit(solution)/shard_map/pallas_call | solution.py:360
  93.7 0.0 copy-done.2
  93.7 0.8 copy.13
Async XLA Ops:
  0.6 2.2 %copy-start.1 = (bf16[2,4,90,512]{3,1,2,0:T(4,128)(2,1)S(1)}, bf16[2,4,90,512]{3,1,2,0:T(4,128)(2,1)}, u32[]{:S(2)}) copy-start(bf16[2,4,90,512]{3,1,2,0:T(4,128)(2,1)} %param.7) | copy-start | bytes 2211844
  89.6 2.7 %copy-start = (bf16[2,4,90,512]{3,2,1,0:T(8,128)(2,1)S(1)}, bf16[2,4,90,512]{3,2,1,0:T(8,128)(2,1)}, u32[]{:S(2)}) copy-start(bf16[2,4,90,512]{3,2,1,0:T(8,128)(2,1)} %get-tuple-element.4) | copy-start | bytes 2211844
  92.3 1.4 %copy-start.2 = (f32[256,512]{1,0:T(8,128)S(1)}, f32[256,512]{1,0:T(8,128)}, u32[]{:S(2)}) copy-start(f32[256,512]{1,0:T(8,128)} %get-tuple-element.11) | copy-start | bytes 1572868

commit v2 on v1

--- a/solution.py
+++ b/solution.py
@@ -49,18 +49,33 @@
             strip[pl.ds(k * padded, padded), pl.ds(first, step)] = jnp.where(inside, hat, 0.0).astype(BF)
 
 
+def spread(block, padded, rows):
+    to = lax.broadcasted_iota(jnp.int32, (rows * padded, block * rows), 0)
+    source = lax.broadcasted_iota(jnp.int32, (rows * padded, block * rows), 1)
+    row = sum((to >= padded * r).astype(jnp.int32) for r in range(1, rows))
+    place = to - padded * row
+    return ((source == place * rows + row) & (place < block)).astype(F32).astype(BF)
+
+
+def gather_back(block, padded, rows):
+    to = lax.broadcasted_iota(jnp.int32, (block * rows, rows * padded), 0)
+    source = lax.broadcasted_iota(jnp.int32, (block * rows, rows * padded), 1)
+    place = lax.div(to, rows)
+    return (source == (to - place * rows) * padded + place).astype(F32).astype(BF)
+
+
 def kernel(
     count, groups,
     f_ref, g_ref, w_ref, width_ref, start_ref,
     out_ref, gi_ref, gw_ref,
     f_send, g_send, f_ext, g_ext, f_strip, g_strip, resp, adj, w_all,
     out_own, gi_own, out_in, gi_in,
-    gw_own, gw_half, gw_mate, gw_sum, gw_ens, gw_lon, gw_lon_in, gw_full,
+    gw_own, gw_half, gw_mate, gw_sum, gw_line, gw_part, gw_part_in, gw_full,
     f_ss, f_rs, f_fs, g_ss, g_rs, g_fs, w_ss, w_rs, w_ms, w_mr,
     out_ss, out_rs, gi_ss, gi_rs,
     a_ss, a_rs, b_ss, b_rs, c_ss, c_rs, d_ss, d_rs,
 ):
-    members, rows, block, channels = f_ref.shape
+    members, block, rows, channels = f_ref.shape
     padded = f_send.shape[1]
     tasks = members * rows
     lon = lax.axis_index("lon")
@@ -68,6 +83,10 @@
     half = lax.rem(lon, 2)
     task = lax.div(lon, 2)
     mate = lon + 1 - 2 * half
+    side = lax.rem(ens, 2)
+    line = lax.div(ens, 2)
+    lines = groups // 2
+    across = ens + 1 - 2 * side
 
     barrier = pltpu.get_barrier_semaphore()
 
@@ -76,32 +95,46 @@
         pl.semaphore_signal(barrier, inc=1, device_id={"lon": lax.rem(lon + o, count), "ens": ens},
                             device_id_type=pl.DeviceIdType.MESH)
 
-    @pl.loop(1, groups)
-    def _(o):
-        pl.semaphore_signal(barrier, inc=1, device_id={"lon": lon, "ens": lax.rem(ens + o, groups)},
+    @pl.loop(1, lines)
+    def _(o):
+        pl.semaphore_signal(barrier, inc=1, device_id={"lon": lon, "ens": 2 * lax.rem(line + o, lines) + side},
                             device_id_type=pl.DeviceIdType.MESH)
 
+    @pl.loop(0, tasks)
+    def _(q):
+        pl.semaphore_signal(barrier, inc=1, device_id={"lon": 2 * q + half, "ens": across},
+                            device_id_type=pl.DeviceIdType.MESH)
+
     def stage(ref, buffer, ext):
-        for q in range(tasks):
-            buffer[q, pl.ds(padded - 16, 16), :] = jnp.zeros((16, channels), BF)
-            buffer[q, pl.ds(0, block), :] = ref[q // rows, q % rows]
+        for m in range(members):
+            flat = ref[m].reshape(block * rows, channels)
+            moved = jnp.dot(to_rows, flat, preferred_element_type=F32).astype(BF)
+            buffer[pl.ds(m * rows, rows)] = moved.reshape(rows, padded, channels)
         ext[lon] = buffer[task]
 
     piece = w_ref.shape[0] // 2
     w_all[ens, 0] = w_ref[0:piece]
     w_all[ens, 1] = w_ref[piece:]
+    to_rows = spread(block, padded, rows)
     stage(g_ref, g_send, g_ext)
     stage(f_ref, f_send, f_ext)
 
-    pl.semaphore_wait(barrier, count - 1 + groups - 1)
+    pl.semaphore_wait(barrier, count - 1 + lines - 1 + tasks)
+
+    w_across = remote(w_all.at[ens, half], w_all.at[ens, half], w_ss.at[0], w_rs.at[ens], lon, across)
+
+    def along(o):
+        return 2 * lax.rem(line + o, lines) + side
 
     def w_copy(o):
-        return remote(w_all.at[ens, half], w_all.at[ens, half], w_ss.at[o], w_rs.at[ens],
-                      lon, lax.rem(ens + o, groups))
+        return remote(w_all.at[ens, half], w_all.at[ens, half], w_ss.at[o], w_rs.at[ens], lon, along(o))
+
+    def w_second(o):
+        return remote(w_all.at[across, half], w_all.at[across, half], w_ss.at[lines + o], w_rs.at[across], lon, along(o))
 
     def w_from(o):
         other = lax.rem(ens + groups - o, groups)
-        return remote(w_all.at[other, half], w_all.at[other, half], w_ss.at[o], w_rs.at[other], lon, other)
+        return remote(w_all.at[other, half], w_all.at[other, half], w_ss.at[0], w_rs.at[other], lon, other)
 
     def in_copy(buffer, ext, ss, rs, o):
         q = lax.rem(task + o, tasks)
@@ -119,7 +152,9 @@
         slot = 2 * lax.rem(task + tasks - o, tasks) + 1 - half
         return remote(ext.at[slot], ext.at[slot], fs.at[o], rs.at[slot], mate, ens)
 
-    @pl.loop(1, groups)
+    w_across.start()
+
+    @pl.loop(1, lines)
     def _(o):
         w_copy(o).start()
 
@@ -133,6 +168,12 @@
 
     forward(g_ext, g_fs, g_rs, 0).start()
     forward(f_ext, f_fs, f_rs, 0).start()
+
+    remote(w_all.at[across, half], w_all.at[across, half], w_ss.at[0], w_rs.at[across], lon, across).wait_recv()
+
+    @pl.loop(1, lines)
+    def _(o):
+        w_second(o).start()
 
     row = lax.rem(task, rows)
     fill_strip(g_strip, width_ref[row], start_ref[row], block, padded, count, True)
@@ -160,10 +201,8 @@
             for k in range(K):
                 result[k, n] = total[k * padded:(k + 1) * padded].astype(BF)
 
-    per = groups // K
-
     def weight_of(k):
-        return w_all[pl.ds(k * per, per)].reshape(channels, channels)
+        return w_all[pl.ds(2 * k, 2)].reshape(channels, channels)
 
     def back_copy(own, into, ss, rs, n):
         return remote(own.at[n], into.at[task], ss.at[n], rs.at[task], 2 * n + half, ens)
@@ -190,7 +229,9 @@
 
     @pl.loop(1, groups)
     def _(o):
-        w_from(o).wait_recv()
+        @pl.when(lax.rem(ens + groups - o, groups) != across)
+        def _():
+            w_from(o).wait_recv()
 
     w_mate = remote(w_all.at[:, half], w_all.at[:, half], w_ms, w_mr, mate, ens)
     w_mate.start()
@@ -201,64 +242,66 @@
     arrive(f_ext, f_ss, f_fs, f_rs)
     own_rows = jnp.concatenate([f_ext[2 * n + half] for n in range(tasks)], axis=0)
     turned = own_rows.T
-    for k in range(K):
-        term = jnp.dot(turned, adj[k].reshape(tasks * padded, channels), preferred_element_type=F32)
-        gw_own[pl.ds(k * per, per)] = term.reshape(per, 2, piece, channels)
-    gw_half[...] = gw_own[:, 1 - half].astype(BF)
-    a_copy = remote(gw_half, gw_mate, a_ss, a_rs, mate, ens)
-    a_copy.start()
+
+    def a_copy(o):
+        to = lax.rem(line + o, lines)
+        return remote(gw_half.at[to], gw_mate.at[to], a_ss.at[o], a_rs.at[to], mate, ens)
+
+    def a_from(o):
+        to = lax.rem(line + o, lines)
+        return remote(gw_half.at[to], gw_mate.at[to], a_ss.at[o], a_rs.at[to], mate, ens)
+
+    @pl.loop(1, lines + 1)
+    def _(o):
+        to = lax.rem(line + o, lines)
+        term = jnp.dot(turned, adj[to].reshape(tasks * padded, channels), preferred_element_type=F32)
+        gw_own[to] = term.reshape(2, 2, piece, channels)
+        gw_half[to] = gw_own[to, :, 1 - half].astype(BF)
+        a_copy(o).start()
+
+    def b_copy(o):
+        to = lax.rem(line + o, lines)
+        return remote(gw_sum.at[to], gw_line.at[line], b_ss.at[o], b_rs.at[line], lon, along(o))
+
+    def b_from(o):
+        other = lax.rem(line + lines - o, lines)
+        return remote(gw_sum.at[other], gw_line.at[other], b_ss.at[o], b_rs.at[other], lon, 2 * other + side)
+
+    @pl.loop(1, lines)
+    def _(o):
+        to = lax.rem(line + o, lines)
+        a_from(o).wait_recv()
+        gw_sum[to] = (gw_own[to, :, half] + gw_mate[to].astype(F32)).astype(BF)
+        b_copy(o).start()
+
+    a_from(lines).wait_recv()
 
     convolve(f_strip, f_ext, resp)
-
-    a_copy.wait_recv()
-    gw_sum[...] = (gw_own[:, half] + gw_mate[...].astype(F32)).astype(BF)
-
-    def b_copy(o):
-        other = lax.rem(ens + o, groups)
-        return remote(gw_sum.at[other], gw_ens.at[ens], b_ss.at[o], b_rs.at[ens], lon, other)
-
-    def b_from(o):
-        other = lax.rem(ens + groups - o, groups)
-        return remote(gw_sum.at[other], gw_ens.at[other], b_ss.at[o], b_rs.at[other], lon, other)
-
-    @pl.loop(1, groups)
-    def _(o):
-        b_copy(o).start()
-
-    gw_ens[ens] = gw_sum[ens]
     mix(resp, out_own, out_in, out_ss, out_rs, False)
 
-    @pl.loop(1, groups)
-    def _(o):
+    total = gw_own[line, :, half] + gw_mate[line].astype(F32)
+    for o in range(1, lines):
         b_from(o).wait_recv()
-
-    total = gw_ens[0].astype(F32)
-    for e in range(1, groups):
-        total = total + gw_ens[e].astype(F32)
-    gw_lon[...] = total.astype(BF).reshape(gw_lon.shape)
+        total = total + gw_line[lax.rem(line + lines - o, lines)].astype(F32)
+    gw_part[...] = total.astype(BF).reshape(gw_part.shape)
+
+    def c_place(o):
+        s = lax.rem(side + lax.div(o, tasks), 2)
+        return s, lax.rem(task + lax.rem(o, tasks), tasks)
 
     def c_copy(o):
-        q = lax.rem(task + o, tasks)
-        return remote(gw_lon.at[q], gw_lon_in.at[task], c_ss.at[o], c_rs.at[task], 2 * q + half, ens)
+        s, q = c_place(o)
+        return remote(gw_part.at[s, q], gw_part_in.at[side, task], c_ss.at[o], c_rs.at[side, task], 2 * q + half, 2 * line + s)
 
     def c_from(o):
-        q = lax.rem(task + tasks - o, tasks)
-        return remote(gw_lon.at[q], gw_lon_in.at[q], c_ss.at[o], c_rs.at[q], 2 * q + half, ens)
-
-    @pl.loop(1, tasks)
+        s, q = c_place(o)
+        return remote(gw_part.at[s, q], gw_part_in.at[s, q], c_ss.at[o], c_rs.at[s, q], 2 * q + half, 2 * line + s)
+
+    @pl.loop(1, 2 * tasks)
     def _(o):
         c_copy(o).start()
 
-    gw_lon_in[task] = gw_lon[task]
-
-    @pl.loop(1, tasks)
-    def _(o):
-        c_from(o).wait_recv()
-
-    total = gw_lon_in[0].astype(F32)
-    for q in range(1, tasks):
-        total = total + gw_lon_in[q].astype(F32)
-    gw_full[lon] = total
+    gw_part_in[side, task] = gw_part[side, task]
 
     def d_copy(o):
         return remote(gw_full.at[lon], gw_full.at[lon], d_ss.at[o], d_rs.at[lon], lax.rem(lon + o, count), ens)
@@ -267,19 +310,35 @@
         other = lax.rem(lon + count - o, count)
         return remote(gw_full.at[other], gw_full.at[other], d_ss.at[o], d_rs.at[other], other, ens)
 
-    @pl.loop(1, count)
-    def _(o):
-        d_copy(o).start()
-
     def finish(ref, own, into, ss, rs):
         into[task] = own[task]
+        for m in range(members):
+            for q in range(m * rows, (m + 1) * rows):
+                @pl.when(q != task)
+                def _():
+                    back_from(own, into, ss, rs, q).wait_recv()
+            flat = into[pl.ds(m * rows, rows)].reshape(rows * padded, channels)
+            moved = jnp.dot(to_places, flat, preferred_element_type=F32).astype(BF)
+            ref[m] = moved.reshape(block, rows, channels)
+
+    to_places = gather_back(block, padded, rows)
+    finish(gi_ref, gi_own, gi_in, gi_ss, gi_rs)
+
+    @pl.loop(1, 2 * tasks)
+    def _(o):
+        c_from(o).wait_recv()
+
+    total = None
+    for e in range(2):
         for q in range(tasks):
-            @pl.when(q != task)
-            def _():
-                back_from(own, into, ss, rs, q).wait_recv()
-            ref[q // rows, q % rows] = into[q, pl.ds(0, block), :]
-
-    finish(gi_ref, gi_own, gi_in, gi_ss, gi_rs)
+            term = gw_part_in[e, q].astype(F32)
+            total = term if total is None else total + term
+    gw_full[lon] = total.astype(BF)
+
+    @pl.loop(1, count)
+    def _(o):
+        d_copy(o).start()
+
     finish(out_ref, out_own, out_in, out_ss, out_rs)
 
     @pl.loop(1, count)
@@ -289,15 +348,24 @@
     strip_rows = gw_full.shape[1]
     for q in range(tasks):
         for s in range(2):
-            gw_ref[pl.ds(s * piece + q * strip_rows, strip_rows), :] = gw_full[2 * q + s]
-
-    @pl.loop(1, groups)
+            gw_ref[pl.ds(s * piece + q * strip_rows, strip_rows), :] = gw_full[2 * q + s].astype(F32)
+
+    w_across.wait_send()
+    w_mate.wait_send()
+
+    @pl.loop(1, lines)
     def _(o):
         w_copy(o).wait_send()
+        w_second(o).wait_send()
         b_copy(o).wait_send()
 
-    w_mate.wait_send()
-    a_copy.wait_send()
+    @pl.loop(1, lines + 1)
+    def _(o):
+        a_copy(o).wait_send()
+
+    @pl.loop(1, 2 * tasks)
+    def _(o):
+        c_copy(o).wait_send()
 
     @pl.loop(0, tasks)
     def _(o):
@@ -308,7 +376,6 @@
     def _(o):
         in_copy(g_send, g_ext, g_ss, g_rs, o).wait_send()
         in_copy(f_send, f_ext, f_ss, f_rs, o).wait_send()
-        c_copy(o).wait_send()
 
     @pl.loop(1, count)
     def _(o):
@@ -322,10 +389,13 @@
 
 
 def on_device(features, weight, grad_out, band_width, band_start):
-    members, rows, block, channels = features.shape
+    features = jnp.transpose(features, (0, 2, 1, 3))
+    grad_out = jnp.transpose(grad_out, (0, 2, 1, 3))
+    members, block, rows, channels = features.shape
     count = lax.axis_size("lon")
     groups = lax.axis_size("ens")
     tasks = members * rows
+    lines = groups // 2
     padded = -(-block // 16) * 16
     shard = weight.shape[0]
     piece = shard // 2
@@ -340,24 +410,24 @@
         field, field, ext, ext, strip, strip, wide, wide,
         vmem((groups, 2, piece, channels), BF),
         field, field, field, field,
-        vmem((groups, 2, piece, channels), F32),
-        vmem((groups, piece, channels), BF),
-        vmem((groups, piece, channels), BF),
-        vmem((groups, piece, channels), BF),
-        vmem((groups, piece, channels), BF),
-        vmem((tasks, strip_rows, channels), BF),
-        vmem((tasks, strip_rows, channels), BF),
-        vmem((count, strip_rows, channels), F32),
+        vmem((lines, 2, 2, piece, channels), F32),
+        vmem((lines, 2, piece, channels), BF),
+        vmem((lines, 2, piece, channels), BF),
+        vmem((lines, 2, piece, channels), BF),
+        vmem((lines, 2, piece, channels), BF),
+        vmem((2, tasks, strip_rows, channels), BF),
+        vmem((2, tasks, strip_rows, channels), BF),
+        vmem((count, strip_rows, channels), BF),
         dma((tasks,)), dma((count,)), dma((tasks,)),
         dma((tasks,)), dma((count,)), dma((tasks,)),
-        dma((groups,)), dma((groups,)), dma(()), dma(()),
+        dma((2 * lines,)), dma((groups,)), dma(()), dma(()),
         dma((tasks,)), dma((tasks,)), dma((tasks,)), dma((tasks,)),
-        dma(()), dma(()), dma((groups,)), dma((groups,)),
-        dma((tasks,)), dma((tasks,)), dma((count,)), dma((count,)),
+        dma((lines + 1,)), dma((lines,)), dma((lines,)), dma((lines,)),
+        dma((2 * tasks,)), dma((2, tasks)), dma((count,)), dma((count,)),
     ]
     whole = pl.BlockSpec(memory_space=pltpu.VMEM)
     scalar = pl.BlockSpec(memory_space=pltpu.SMEM)
-    return pl.pallas_call(
+    output, grad_input, grad_weight = pl.pallas_call(
         functools.partial(kernel, count, groups),
         out_shape=(
             jax.ShapeDtypeStruct(features.shape, BF),
@@ -371,6 +441,7 @@
             collective_id=0, has_side_effects=True, vmem_limit_bytes=60 * 1024 * 1024
         ),
     )(features, grad_out, weight, band_width, band_start)
+    return jnp.transpose(output, (0, 2, 1, 3)), jnp.transpose(grad_input, (0, 2, 1, 3)), grad_weight
 
 
 def solution(mesh):

time: 94.7 us -> 76.5 us (0.81)
  Pallas kernels: 85.7 us -> 71.2 us
  local copies, waits for them, and re-layouts: 8.12 us -> 4.41 us
    pallas_call x1, Pallas kernels: 85.7 us -> 71.2 us  [on_device(): pl.pallas_call(functools.partial(kernel, count, groups), out_shape=(jax.S...]
    pallas_call x2 -> x0, local copies, waits for them, and re-layouts: 4.07 us -> none  [on_device(): pl.pallas_call(functools.partial(kernel, count, groups), out_shape=(jax.S...]
    unnamed x9 -> x7, local copies, waits for them, and re-layouts: 4.05 us -> 4.41 us
where the time goes in v2:
time: 76.5 us; the launch traced here: 76.2 us
  Pallas kernels  71.2 us (93%)
  local copies, waits for them, and re-layouts  4.41 us (6%)
    pallas_call x1, Pallas kernels, on_device(): pl.pallas_call(functools.partial(kernel, count, groups), out_shape=(jax.S...  71.2 us
    unnamed x7, local copies, waits for them, and re-layouts  4.41 us

profile of v2, /device:TPU:1, one launch (start us, length us, event | category | flops | bytes accessed | tf_op | source)
XLA Modules:
  0.0 76.2 jit_solution(8859610668542057358)
XLA Ops:
  0.6 71.2 %shard_map.76 = (bf16[2,90,4,512]{3,2,1,0:T(4,128)(2,1)}, bf16[2,90,4,512]{3,2,1,0:T(4,128)(2,1)}, f32[256,512]{1,0:T(8,128)}) custom-call(bf16[2,90,4,512]{3,2,1,0:T(4,128)(2,1)} %bitcast.4, bf16[2,90,4,512]{3,2,1,0:T(4,128)(2,1)} %bitcast.5, bf16[256,512]{1,0:T(8,128)(2,1)} %w_ref.1, s32[4]{0:T(128)} %width_ref.1, s32[4]{0:T(128)} %start_ref.1), custom_call_target="tpu_custom_call" | custom-call | tf_op jit(solution)/shard_map/pallas_call | solution.py:430
  71.8 0.0 copy-start
  71.8 2.3 %copy.11 = bf16[2,4,90,512]{3,1,2,0:T(4,128)(2,1)} copy(bf16[2,4,90,512]{3,1,2,0:T(4,128)(2,1)} %bitcast.7) | data formatting | bytes 1474560
  74.1 0.0 copy-done
  74.1 0.0 copy-start.1
  74.1 0.9 %copy.12 = bf16[2,4,90,512]{3,1,2,0:T(4,128)(2,1)} copy(bf16[2,4,90,512]{3,1,2,0:T(4,128)(2,1)S(1)} %bitcast.6) | data formatting | bytes 1474560
  75.0 0.4 copy-done.1
  75.5 0.8 %copy.13 = f32[256,512]{1,0:T(8,128)} copy(f32[256,512]{1,0:T(8,128)S(1)} %copy-done.1) | data formatting | bytes 1048576
Async XLA Ops:
  71.8 2.3 %copy-start = (bf16[2,90,4,512]{3,2,1,0:T(4,128)(2,1)S(1)}, bf16[2,90,4,512]{3,2,1,0:T(4,128)(2,1)}, u32[]{:S(2)}) copy-start(bf16[2,90,4,512]{3,2,1,0:T(4,128)(2,1)} %get-tuple-element.7) | copy-start | bytes 2211844
  74.1 1.3 %copy-start.1 = (f32[256,512]{1,0:T(8,128)S(1)}, f32[256,512]{1,0:T(8,128)}, u32[]{:S(2)}) copy-start(f32[256,512]{1,0:T(8,128)} %get-tuple-element.14) | copy-start | bytes 1572868

commit v3 on v2

v3 whole, which is shorter than its diff:
```python
import functools

import jax
import jax.numpy as jnp
from jax import lax
from jax.experimental import pallas as pl
from jax.experimental.pallas import tpu as pltpu
from jax.sharding import PartitionSpec as P

K = 4
BF = jnp.bfloat16
F32 = jnp.float32


def remote(src, dst, send, recv, lon, ens):
    return pltpu.make_async_remote_copy(
        src_ref=src,
        dst_ref=dst,
        send_sem=send,
        recv_sem=recv,
        device_id={"lon": lon, "ens": ens},
        device_id_type=pl.DeviceIdType.MESH,
    )


def fill_strips(plus, minus, width, start, block, padded, count, flip):
    circle = block * count
    lanes = padded * count // 2
    step = min(128, lanes)
    row = lax.broadcasted_iota(jnp.int32, (padded, step), 0)
    lane = lax.broadcasted_iota(jnp.int32, (padded, step), 1)
    wide = jnp.full((1, step), width.astype(F32), F32)
    scale = 0.5 / jnp.sqrt(wide)
    for first in range(0, lanes, step):
        column = lane + first
        low = first // padded
        part = jnp.full_like(column, low)
        for edge in range(low + 1, (first + step - 1) // padded + 1):
            part = part + (column >= edge * padded).astype(jnp.int32)
        inner = column - part * padded
        place = inner + part * block
        valid = (inner < block) & (row < block)
        near = (row - place if flip else place - row) - start
        near = jnp.where(near < 0, near + circle, near)
        near = jnp.where(near >= circle, near - circle, near)
        far = jnp.where(near >= circle // 2, near - circle // 2, near + circle // 2)
        in_near = valid & (near < width)
        in_far = valid & (far < width)
        at_near = (near.astype(F32) + 0.5) * (K - 1) / wide
        at_far = (far.astype(F32) + 0.5) * (K - 1) / wide
        for k in range(K):
            one = jnp.where(in_near, jnp.maximum(0.0, 1.0 - jnp.abs(at_near - float(k))) * scale, 0.0)
            two = jnp.where(in_far, jnp.maximum(0.0, 1.0 - jnp.abs(at_far - float(k))) * scale, 0.0)
            where = (pl.ds(k * padded, padded), pl.ds(first, step))
            plus[where] = (one + two).astype(BF)
            minus[where] = (one - two).astype(BF)


def spread(block, padded, rows):
    to = lax.broadcasted_iota(jnp.int32, (rows * padded, block * rows), 0)
    source = lax.broadcasted_iota(jnp.int32, (rows * padded, block * rows), 1)
    row = sum((to >= padded * r).astype(jnp.int32) for r in range(1, rows))
    place = to - padded * row
    return ((source == place * rows + row) & (place < block)).astype(F32).astype(BF)


def gather_back(block, padded, rows):
    to = lax.broadcasted_iota(jnp.int32, (block * rows, rows * padded), 0)
    source = lax.broadcasted_iota(jnp.int32, (block * rows, rows * padded), 1)
    place = lax.div(to, rows)
    return (source == (to - place * rows) * padded + place).astype(F32).astype(BF)


def kernel(
    count, groups,
    f_hbm, g_hbm, w_hbm, width_ref, start_ref,
    out_in, gi_in, gw_ref,
    f_ref, g_ref, f_send, g_send, f_ext, g_ext, f_plus, f_minus, g_plus, g_minus, sums, differences, resp, adj, w_all,
    out_own, gi_own,
    turned, gw_own, gw_half, gw_mate, gw_sum, gw_hop, gw_line, gw_part, gw_part_in, gw_full,
    f_ss, f_rs, f_fs, g_ss, g_rs, g_fs, w_ss, w_rs, w_ms, w_mr,
    out_ss, out_rs, gi_ss, gi_rs,
    a_ss, a_rs, b_ss, b_hs, b_rs, c_ss, c_rs, d_ss, d_rs, d_ms, keep_sem, load_sem,
):
    members, block, rows, channels = f_hbm.shape
    padded = f_send.shape[1]
    tasks = members * rows
    lon = lax.axis_index("lon")
    ens = lax.axis_index("ens")
    half = lax.rem(lon, 2)
    task = lax.div(lon, 2)
    mate = lon + 1 - 2 * half
    side = lax.rem(ens, 2)
    line = lax.div(ens, 2)
    lines = groups // 2
    across = ens + 1 - 2 * side
    beside = lon + 2 - 4 * lax.rem(task, 2)

    barrier = pltpu.get_barrier_semaphore()

    def greet(to_lon, to_ens):
        pl.semaphore_signal(barrier, inc=1, device_id={"lon": to_lon, "ens": to_ens}, device_id_type=pl.DeviceIdType.MESH)

    for o in range(1, tasks):
        greet(2 * lax.rem(task + o, tasks) + half, ens)
    greet(mate, ens)
    for o in range(1, lines):
        greet(lon, 2 * lax.rem(line + o, lines) + side)
    for o in range(tasks):
        greet(2 * lax.rem(task + o, tasks) + half, across)

    def stage(ref, buffer, ext):
        for m in range(members):
            flat = ref[m].reshape(block * rows, channels)
            moved = jnp.dot(to_rows, flat, preferred_element_type=F32).astype(BF)
            buffer[pl.ds(m * rows, rows)] = moved.reshape(rows, padded, channels)
        ext[lon] = buffer[task]

    piece = w_all.shape[2]
    load_g = pltpu.make_async_copy(g_hbm, g_ref, load_sem.at[0])
    load_w = [pltpu.make_async_copy(w_hbm.at[pl.ds(i * piece, piece)], w_all.at[ens, i], load_sem.at[1 + i]) for i in range(2)]
    load_f = pltpu.make_async_copy(f_hbm, f_ref, load_sem.at[3])
    for load in (load_g, *load_w, load_f):
        load.start()
    to_rows = spread(block, padded, rows)
    load_g.wait()
    stage(g_ref, g_send, g_ext)
    for load in load_w:
        load.wait()

    pl.semaphore_wait(barrier, 2 * tasks + lines - 1)

    w_across = remote(w_all.at[ens, half], w_all.at[ens, half], w_ss.at[0], w_rs.at[ens], beside, across)

    def along(o):
        return 2 * lax.rem(line + o, lines) + side

    def w_copy(o):
        return remote(w_all.at[ens, half], w_all.at[ens, half], w_ss.at[o], w_rs.at[ens], lon, along(o))

    def w_second(o):
        return remote(w_all.at[across, half], w_all.at[across, half], w_ss.at[lines + o], w_rs.at[across], lon, along(o))

    def w_from(other):
        return remote(w_all.at[other, half], w_all.at[other, half], w_ss.at[0], w_rs.at[other], lon, other)

    def in_copy(buffer, ext, ss, rs, o):
        q = lax.rem(task + o, tasks)
        return remote(buffer.at[q], ext.at[lon], ss.at[o], rs.at[lon], 2 * q + half, ens)

    def in_from(ext, ss, rs, o):
        slot = 2 * lax.rem(task + tasks - o, tasks) + half
        return remote(ext.at[slot], ext.at[slot], ss.at[o], rs.at[slot], slot, ens)

    def forward(ext, fs, rs, o):
        slot = 2 * lax.rem(task + tasks - o, tasks) + half
        return remote(ext.at[slot], ext.at[slot], fs.at[o], rs.at[slot], mate, ens)

    def forwarded(ext, fs, rs, o):
        slot = 2 * lax.rem(task + tasks - o, tasks) + 1 - half
        return remote(ext.at[slot], ext.at[slot], fs.at[o], rs.at[slot], mate, ens)

    @pl.loop(1, tasks)
    def _(o):
        in_copy(g_send, g_ext, g_ss, g_rs, o).start()

    w_across.start()

    @pl.loop(1, lines)
    def _(o):
        w_copy(o).start()

    forward(g_ext, g_fs, g_rs, 0).start()
    load_f.wait()
    stage(f_ref, f_send, f_ext)
    forward(f_ext, f_fs, f_rs, 0).start()

    remote(w_all.at[across, half], w_all.at[across, half], w_ss.at[0], w_rs.at[across], beside, across).wait_recv()

    @pl.loop(1, lines)
    def _(o):
        w_second(o).start()

    row = lax.rem(task, rows)
    fill_strips(g_plus, g_minus, width_ref[row], start_ref[row], block, padded, count, True)

    @pl.loop(1, tasks)
    def _(o):
        in_copy(g_send, g_ext, g_ss, g_rs, o).wait_send()
        in_copy(f_send, f_ext, f_ss, f_rs, o).start()

    fill_strips(f_plus, f_minus, width_ref[row], start_ref[row], block, padded, count, False)

    def pass_on(ext, ss, fs, rs):
        @pl.loop(1, tasks)
        def _(o):
            in_from(ext, ss, rs, o).wait_recv()
            forward(ext, fs, rs, o).start()

    def complete(ext, fs, rs):
        @pl.loop(0, tasks)
        def _(o):
            forwarded(ext, fs, rs, o).wait_recv()

        @pl.loop(0, tasks)
        def _(b):
            one = ext[b].astype(F32)
            two = ext[tasks + b].astype(F32)
            both = (one + two).astype(BF)
            apart = one - two
            sums[b] = both
            sums[tasks + b] = both
            differences[b] = apart.astype(BF)
            differences[tasks + b] = (-apart).astype(BF)

    def convolve(plus, minus, result):
        @pl.loop(0, tasks // 2)
        def _(n):
            window = pl.ds(2 * n + half, tasks)
            both = jnp.dot(plus[...], sums[window].reshape(tasks * padded, channels), preferred_element_type=F32)
            apart = jnp.dot(minus[...], differences[window].reshape(tasks * padded, channels), preferred_element_type=F32)
            near = (both + apart).astype(BF)
            far = (both - apart).astype(BF)
            for k in range(K):
                result[k, n] = near[k * padded:(k + 1) * padded]
                result[k, tasks // 2 + n] = far[k * padded:(k + 1) * padded]

    def weight_of(k):
        return w_all[pl.ds(2 * k, 2)].reshape(channels, channels)

    def back_copy(own, into, ss, rs, n):
        return remote(own.at[n], into.at[task], ss.at[n], rs.at[task], 2 * n + half, ens)

    def back_from(own, into, ss, rs, n):
        return remote(own.at[n], into.at[n], ss.at[n], rs.at[n], 2 * n + half, ens)

    def mix(source, own, c, flip):
        chunk = tasks // 2
        total = None
        for k in range(K):
            part = source[k, pl.ds(c * chunk, chunk)].reshape(chunk * padded, channels)
            dims = (((1,), (1 if flip else 0,)), ((), ()))
            term = lax.dot_general(part, weight_of(k), dims, preferred_element_type=F32)
            total = term if total is None else total + term
        own[pl.ds(c * chunk, chunk)] = total.astype(BF).reshape(chunk, padded, channels)

    def send_back(own, into, ss, rs, c):
        chunk = tasks // 2
        for n in range(c * chunk, (c + 1) * chunk):
            @pl.when(n != task)
            def _():
                back_copy(own, into, ss, rs, n).start()

    pass_on(g_ext, g_ss, g_fs, g_rs)
    complete(g_ext, g_fs, g_rs)

    def w_mate(e):
        return remote(w_all.at[e, half], w_all.at[e, half], w_ms.at[e], w_mr.at[e], mate, ens)

    def w_mate_from(e):
        return remote(w_all.at[e, 1 - half], w_all.at[e, 1 - half], w_ms.at[e], w_mr.at[e], mate, ens)

    @pl.loop(1, lines)
    def _(o):
        w_from(along(o)).wait_recv()
        w_mate(along(o)).start()

    w_mate(across).start()
    convolve(g_plus, g_minus, adj)

    @pl.loop(1, lines)
    def _(o):
        w_from(along(o) + 1 - 2 * side).wait_recv()
        w_mate(along(o) + 1 - 2 * side).start()

    @pl.loop(1, groups)
    def _(o):
        w_mate_from(lax.rem(ens + o, groups)).wait_recv()

    for c in range(2):
        mix(adj, gi_own, c, True)
        send_back(gi_own, gi_in, gi_ss, gi_rs, c)

    pass_on(f_ext, f_ss, f_fs, f_rs)
    own_rows = jnp.concatenate([f_ext[2 * n + half] for n in range(tasks)], axis=0)
    turned[...] = own_rows.T.reshape(turned.shape)

    def a_copy(to):
        return remote(gw_half.at[to], gw_mate.at[to], a_ss.at[to], a_rs.at[to], mate, ens)

    def terms(to, which):
        left = turned[:, which].reshape(2 * piece, tasks * padded)
        right = adj[to].reshape(tasks * padded, channels)
        return jnp.dot(left, right, preferred_element_type=F32).reshape(2, piece, channels)

    order = [lax.rem(line + o, lines) for o in (2, 1, 3, 0)]
    for to in order:
        gw_half[to] = terms(to, 1 - half).astype(BF)
        a_copy(to).start()
    for to in order:
        gw_own[to] = terms(to, half)

    ahead = lax.rem(line + 1, lines)
    back = lax.rem(line + lines - 1, lines)
    opposite = lax.rem(line + 2, lines)
    ways = ((0, ahead, back), (1, back, ahead))

    def chip_sum(to, i):
        return gw_own[to, i] + gw_mate[to, i].astype(F32)

    def hop(i):
        _, to, _ = ways[i]
        return remote(gw_sum.at[opposite, i], gw_hop.at[i], b_ss.at[0, i], b_hs.at[i], lon, 2 * to + side)

    def plain(i):
        _, to, _ = ways[i]
        return remote(gw_sum.at[to, 1 - i], gw_line.at[i, 1 - i], b_ss.at[1, i], b_rs.at[i, 1 - i], lon, 2 * to + side)

    def added(i):
        _, to, _ = ways[i]
        return remote(gw_sum.at[to, i], gw_line.at[i, i], b_ss.at[2, i], b_rs.at[i, i], lon, 2 * to + side)

    a_copy(opposite).wait_recv()
    for i in range(2):
        gw_sum[opposite, i] = chip_sum(opposite, i).astype(BF)
        hop(i).start()
    for i, to, _ in ways:
        a_copy(to).wait_recv()
        gw_sum[to, 1 - i] = chip_sum(to, 1 - i).astype(BF)
        plain(i).start()
    a_copy(line).wait_recv()

    complete(f_ext, f_fs, f_rs)
    convolve(f_plus, f_minus, resp)

    for i, to, _ in ways:
        hop(i).wait_recv()
        gw_sum[to, i] = (chip_sum(to, i) + gw_hop[i].astype(F32)).astype(BF)
        added(i).start()

    mix(resp, out_own, 0, False)
    send_back(out_own, out_in, out_ss, out_rs, 0)
    mix(resp, out_own, 1, False)

    for i in range(2):
        plain(i).wait_recv()
        added(i).wait_recv()
    for s in range(2):
        total = chip_sum(line, s) + gw_line[0, s].astype(F32) + gw_line[1, s].astype(F32)
        gw_part[s] = total.astype(BF).reshape(gw_part.shape[1:])

    def c_place(o):
        s = lax.rem(side + lax.div(o, tasks), 2)
        return s, lax.rem(task + lax.rem(o, tasks), tasks)

    def c_copy(o):
        s, q = c_place(o)
        return remote(gw_part.at[s, q], gw_part_in.at[side, task], c_ss.at[o], c_rs.at[side, task], 2 * q + half, 2 * line + s)

    def c_from(o):
        s, q = c_place(o)
        return remote(gw_part.at[s, q], gw_part_in.at[s, q], c_ss.at[o], c_rs.at[s, q], 2 * q + half, 2 * line + s)

    @pl.loop(1, 2 * tasks)
    def _(o):
        c_copy(o).start()

    send_back(out_own, out_in, out_ss, out_rs, 1)
    gw_part_in[side, task] = gw_part[side, task]

    def d_copy(o):
        return remote(gw_full.at[lon], gw_full.at[lon], d_ss.at[o], d_rs.at[lon], 2 * lax.rem(task + o, tasks) + half, ens)

    def d_from(o):
        other = 2 * lax.rem(task + tasks - o, tasks) + half
        return remote(gw_full.at[other], gw_full.at[other], d_ss.at[o], d_rs.at[other], other, ens)

    def d_mate(o):
        other = 2 * lax.rem(task + tasks - o, tasks) + half
        return remote(gw_full.at[other], gw_full.at[other], d_ms.at[o], d_rs.at[other], mate, ens)

    def d_mate_from(o):
        other = 2 * lax.rem(task + tasks - o, tasks) + 1 - half
        return remote(gw_full.at[other], gw_full.at[other], d_ms.at[o], d_rs.at[other], mate, ens)

    @pl.loop(1, 2 * tasks)
    def _(o):
        c_from(o).wait_recv()

    total = None
    for e in range(2):
        for q in range(tasks):
            term = gw_part_in[e, q].astype(F32)
            total = term if total is None else total + term
    gw_full[lon] = total.astype(BF)

    @pl.loop(1, tasks)
    def _(o):
        d_copy(o).start()

    d_mate(0).start()

    keep_gi = pltpu.make_async_copy(gi_own.at[task], gi_in.at[task], keep_sem.at[0])
    keep_out = pltpu.make_async_copy(out_own.at[task], out_in.at[task], keep_sem.at[1])
    keep_gi.start()
    keep_out.start()

    @pl.loop(1, tasks)
    def _(o):
        d_from(o).wait_recv()
        d_mate(o).start()

    @pl.loop(0, tasks)
    def _(o):
        d_mate_from(o).wait_recv()

    gw_ref[...] = gw_full[...]

    for n in range(tasks):
        @pl.when(n != task)
        def _():
            back_from(gi_own, gi_in, gi_ss, gi_rs, n).wait_recv()
            back_from(out_own, out_in, out_ss, out_rs, n).wait_recv()

    keep_gi.wait()
    keep_out.wait()

    w_across.wait_send()

    @pl.loop(1, lines)
    def _(o):
        w_copy(o).wait_send()
        w_second(o).wait_send()

    @pl.loop(1, groups)
    def _(o):
        w_mate(lax.rem(ens + o, groups)).wait_send()

    @pl.loop(0, lines)
    def _(o):
        a_copy(o).wait_send()

    for i in range(2):
        hop(i).wait_send()
        plain(i).wait_send()
        added(i).wait_send()

    @pl.loop(1, 2 * tasks)
    def _(o):
        c_copy(o).wait_send()

    @pl.loop(0, tasks)
    def _(o):
        forward(g_ext, g_fs, g_rs, o).wait_send()
        forward(f_ext, f_fs, f_rs, o).wait_send()

    @pl.loop(1, tasks)
    def _(o):
        in_copy(f_send, f_ext, f_ss, f_rs, o).wait_send()

    @pl.loop(1, tasks)
    def _(o):
        d_copy(o).wait_send()

    @pl.loop(0, tasks)
    def _(o):
        d_mate(o).wait_send()

    for n in range(tasks):
        @pl.when(n != task)
        def _():
            back_copy(gi_own, gi_in, gi_ss, gi_rs, n).wait_send()
            back_copy(out_own, out_in, out_ss, out_rs, n).wait_send()


def lay_out(block, out_hbm, gi_hbm, gw_hbm, out_ref, gi_ref, gw_ref, out_in, gi_in, gw_in, out_done, gi_done, gw_done, sems, done_sems):
    tasks, padded, channels = out_hbm.shape
    members, _, rows, _ = out_ref.shape
    loads = []
    for i, (source, into) in enumerate(((gi_hbm, gi_in), (out_hbm, out_in))):
        for m in range(members):
            part = pl.ds(m * rows, rows)
            loads.append(pltpu.make_async_copy(source.at[part], into.at[part], sems.at[i * members + m]))
    loads.append(pltpu.make_async_copy(gw_hbm, gw_in, sems.at[2 * members]))
    for load in loads:
        load.start()
    to_places = gather_back(block, padded, rows)
    stores = []
    for i, (into, ready, ref) in enumerate(((gi_in, gi_done, gi_ref), (out_in, out_done, out_ref))):
        for m in range(members):
            loads[i * members + m].wait()
            flat = into[pl.ds(m * rows, rows)].reshape(rows * padded, channels)
            moved = jnp.dot(to_places, flat, preferred_element_type=F32).astype(BF)
            ready[m] = moved.reshape(block, rows, channels)
            stores.append(pltpu.make_async_copy(ready.at[m], ref.at[m], done_sems.at[i * members + m]))
            stores[-1].start()
    loads[-1].wait()
    strip_rows = gw_in.shape[1]
    for q in range(tasks):
        for s in range(2):
            gw_done[pl.ds((s * tasks + q) * strip_rows, strip_rows), :] = gw_in[2 * q + s].astype(F32)
    stores.append(pltpu.make_async_copy(gw_done, gw_ref, done_sems.at[2 * members]))
    stores[-1].start()
    for store in stores:
        store.wait()


def on_device(features, weight, grad_out, band_width, band_start):
    features = jnp.transpose(features, (0, 2, 1, 3))
    grad_out = jnp.transpose(grad_out, (0, 2, 1, 3))
    members, block, rows, channels = features.shape
    count = lax.axis_size("lon")
    groups = lax.axis_size("ens")
    tasks = members * rows
    lines = groups // 2
    padded = -(-block // 16) * 16
    shard = weight.shape[0]
    piece = shard // 2
    strip_rows = piece // tasks
    vmem = pltpu.VMEM
    dma = pltpu.SemaphoreType.DMA
    field = vmem((tasks, padded, channels), BF)
    ext = vmem((count, padded, channels), BF)
    strip = vmem((K * padded, tasks * padded), BF)
    wide = vmem((K, tasks, padded, channels), BF)
    scratch = [
        vmem(features.shape, BF), vmem(features.shape, BF), field, field, ext, ext, strip, strip, strip, strip, ext, ext, wide, wide,
        vmem((groups, 2, piece, channels), BF),
        field, field,
        vmem((2, 2, piece, tasks * padded), BF),
        vmem((lines, 2, piece, channels), F32),
        vmem((lines, 2, piece, channels), BF),
        vmem((lines, 2, piece, channels), BF),
        vmem((lines, 2, piece, channels), BF),
        vmem((2, piece, channels), BF),
        vmem((2, 2, piece, channels), BF),
        vmem((2, tasks, strip_rows, channels), BF),
        vmem((2, tasks, strip_rows, channels), BF),
        vmem((count, strip_rows, channels), BF),
        dma((tasks,)), dma((count,)), dma((tasks,)),
        dma((tasks,)), dma((count,)), dma((tasks,)),
        dma((2 * lines,)), dma((groups,)), dma((groups,)), dma((groups,)),
        dma((tasks,)), dma((tasks,)), dma((tasks,)), dma((tasks,)),
        dma((lines,)), dma((lines,)), dma((3, 2)), dma((2,)), dma((2, 2)),
        dma((2 * tasks,)), dma((2, tasks)), dma((tasks,)), dma((count,)), dma((tasks,)), dma((2,)), dma((4,)),
    ]
    whole = pl.BlockSpec(memory_space=pltpu.VMEM)
    scalar = pl.BlockSpec(memory_space=pltpu.SMEM)
    any_place = pl.BlockSpec(memory_space=pl.ANY)
    back = jax.ShapeDtypeStruct((tasks, padded, channels), BF)
    parts = pl.pallas_call(
        functools.partial(kernel, count, groups),
        out_shape=(back, back, jax.ShapeDtypeStruct((count, strip_rows, channels), BF)),
        in_specs=[any_place, any_place, any_place, scalar, scalar],
        out_specs=(any_place, any_place, whole),
        scratch_shapes=scratch,
        compiler_params=pltpu.CompilerParams(
            collective_id=0, has_side_effects=True, vmem_limit_bytes=60 * 1024 * 1024
        ),
    )(features, grad_out, weight, band_width, band_start)
    output, grad_input, grad_weight = pl.pallas_call(
        functools.partial(lay_out, block),
        out_shape=(
            jax.ShapeDtypeStruct(features.shape, BF),
            jax.ShapeDtypeStruct(features.shape, BF),
            jax.ShapeDtypeStruct(weight.shape, F32),
        ),
        in_specs=[any_place] * 3,
        out_specs=(any_place,) * 3,
        scratch_shapes=[
            field, field, vmem((count, strip_rows, channels), BF),
            vmem(features.shape, BF), vmem(features.shape, BF), vmem(weight.shape, F32),
            dma((2 * members + 1,)), dma((2 * members + 1,)),
        ],
        compiler_params=pltpu.CompilerParams(vmem_limit_bytes=60 * 1024 * 1024),
    )(*parts)
    return jnp.transpose(output, (0, 2, 1, 3)), jnp.transpose(grad_input, (0, 2, 1, 3)), grad_weight


def solution(mesh):
    placed = (P("ens", None, "lon", None), P("ens", None), P("ens", None, "lon", None), P(), P())
    return jax.shard_map(
        on_device,
        mesh=mesh,
        in_specs=placed,
        out_specs=(P("ens", None, "lon", None), P("ens", None, "lon", None), P("ens", None)),
        check_vma=False,
    )
```

time: 76.5 us -> 67.6 us (0.88)
  local copies, waits for them, and re-layouts: 4.41 us -> 0 us
  Pallas kernels: 71.2 us -> 66.8 us
    unnamed x7 -> x0, local copies, waits for them, and re-layouts: 4.41 us -> none
    pallas_call x1 -> x2, Pallas kernels: 71.2 us -> 66.8 us  [the longest x1 63.4 us: on_device(): pl.pallas_call(functools.partial(kernel, count, groups), out_shape=(back,...]
where the time goes in v3:
time: 67.6 us; the launch traced here: 67.5 us
  Pallas kernels  66.8 us (99%)
    pallas_call x1, Pallas kernels, on_device(): pl.pallas_call(functools.partial(kernel, count, groups), out_shape=(back,...  63.4 us
    pallas_call x1, Pallas kernels, on_device(): pl.pallas_call(functools.partial(lay_out, block), out_shape=(jax.ShapeDty...  3.44 us

profile of v3, /device:TPU:1, one launch (start us, length us, event | category | flops | bytes accessed | tf_op | source)
XLA Modules:
  0.0 67.5 jit_solution(8317557059036686682)
XLA Ops:
  0.6 63.4 %shard_map.76 = (bf16[8,96,512]{2,1,0:T(8,128)(2,1)}, bf16[8,96,512]{2,1,0:T(8,128)(2,1)}, bf16[16,16,512]{2,1,0:T(8,128)(2,1)}) custom-call(bf16[2,90,4,512]{3,2,1,0:T(4,128)(2,1)} %bitcast.4, bf16[2,90,4,512]{3,2,1,0:T(4,128)(2,1)} %bitcast.5, bf16[256,512]{1,0:T(8,128)(2,1)} %w_hbm.1, s32[4]{0:T(128)} %width_ref.1, s32[4]{0:T(128)} %start_ref.1), custom_call_target="tpu_custom_call" | custom-call | tf_op jit(solution)/shard_map/pallas_call | solution.py:551
  64.0 3.4 %shard_map.77 = (bf16[2,90,4,512]{3,2,1,0:T(4,128)(2,1)}, bf16[2,90,4,512]{3,2,1,0:T(4,128)(2,1)}, f32[256,512]{1,0:T(8,128)}) custom-call(bf16[8,96,512]{2,1,0:T(8,128)(2,1)} %get-tuple-element.9.out_hbm, bf16[8,96,512]{2,1,0:T(8,128)(2,1)} %get-tuple-element.10.gi_hbm, bf16[16,16,512]{2,1,0:T(8,128)(2,1)} %get-tuple-element.11.gw_hbm), custom_call_target="tpu_custom_call" | custom-call | tf_op jit(solution)/shard_map/pallas_call | solution.py:561

commit v4 on v3

--- a/solution.py
+++ b/solution.py
@@ -74,9 +74,9 @@
 def kernel(
     count, groups,
     f_hbm, g_hbm, w_hbm, width_ref, start_ref,
-    out_in, gi_in, gw_ref,
+    out_ref, gi_ref, gw_ref,
     f_ref, g_ref, f_send, g_send, f_ext, g_ext, f_plus, f_minus, g_plus, g_minus, sums, differences, resp, adj, w_all,
-    out_own, gi_own,
+    out_own, gi_own, out_in, gi_in, out_done, gi_done, gw_done,
     turned, gw_own, gw_half, gw_mate, gw_sum, gw_hop, gw_line, gw_part, gw_part_in, gw_full,
     f_ss, f_rs, f_fs, g_ss, g_rs, g_fs, w_ss, w_rs, w_ms, w_mr,
     out_ss, out_rs, gi_ss, gi_rs,
@@ -106,8 +106,7 @@
     greet(mate, ens)
     for o in range(1, lines):
         greet(lon, 2 * lax.rem(line + o, lines) + side)
-    for o in range(tasks):
-        greet(2 * lax.rem(task + o, tasks) + half, across)
+    greet(beside, across)
 
     def stage(ref, buffer, ext):
         for m in range(members):
@@ -128,7 +127,7 @@
     for load in load_w:
         load.wait()
 
-    pl.semaphore_wait(barrier, 2 * tasks + lines - 1)
+    pl.semaphore_wait(barrier, tasks + lines)
 
     w_across = remote(w_all.at[ens, half], w_all.at[ens, half], w_ss.at[0], w_rs.at[ens], beside, across)
 
@@ -294,11 +293,10 @@
         return jnp.dot(left, right, preferred_element_type=F32).reshape(2, piece, channels)
 
     order = [lax.rem(line + o, lines) for o in (2, 1, 3, 0)]
-    for to in order:
+    for to in order[:2]:
         gw_half[to] = terms(to, 1 - half).astype(BF)
         a_copy(to).start()
-    for to in order:
-        gw_own[to] = terms(to, half)
+    gw_own[order[0]] = terms(order[0], half)
 
     ahead = lax.rem(line + 1, lines)
     back = lax.rem(line + lines - 1, lines)
@@ -324,6 +322,11 @@
     for i in range(2):
         gw_sum[opposite, i] = chip_sum(opposite, i).astype(BF)
         hop(i).start()
+    for to in order[2:]:
+        gw_half[to] = terms(to, 1 - half).astype(BF)
+        a_copy(to).start()
+    for to in order[1:]:
+        gw_own[to] = terms(to, half)
     for i, to, _ in ways:
         a_copy(to).wait_recv()
         gw_sum[to, 1 - i] = chip_sum(to, 1 - i).astype(BF)
@@ -383,6 +386,24 @@
         other = 2 * lax.rem(task + tasks - o, tasks) + 1 - half
         return remote(gw_full.at[other], gw_full.at[other], d_ms.at[o], d_rs.at[other], mate, ens)
 
+    def finish(ref, done, own, into, ss, rs, which):
+        into[task] = own[task]
+        keeps = []
+        for m in range(members):
+            for q in range(m * rows, (m + 1) * rows):
+                @pl.when(q != task)
+                def _():
+                    back_from(own, into, ss, rs, q).wait_recv()
+            flat = into[pl.ds(m * rows, rows)].reshape(rows * padded, channels)
+            moved = jnp.dot(to_places, flat, preferred_element_type=F32).astype(BF)
+            done[m] = moved.reshape(block, rows, channels)
+            keeps.append(pltpu.make_async_copy(done.at[m], ref.at[m], keep_sem.at[which * members + m]))
+            keeps[-1].start()
+        return keeps
+
+    to_places = gather_back(block, padded, rows)
+    keep_gi = finish(gi_ref, gi_done, gi_own, gi_in, gi_ss, gi_rs, 0)
+
     @pl.loop(1, 2 * tasks)
     def _(o):
         c_from(o).wait_recv()
@@ -400,10 +421,7 @@
 
     d_mate(0).start()
 
-    keep_gi = pltpu.make_async_copy(gi_own.at[task], gi_in.at[task], keep_sem.at[0])
-    keep_out = pltpu.make_async_copy(out_own.at[task], out_in.at[task], keep_sem.at[1])
-    keep_gi.start()
-    keep_out.start()
+    keep_out = finish(out_ref, out_done, out_own, out_in, out_ss, out_rs, 1)
 
     @pl.loop(1, tasks)
     def _(o):
@@ -414,16 +432,14 @@
     def _(o):
         d_mate_from(o).wait_recv()
 
-    gw_ref[...] = gw_full[...]
-
-    for n in range(tasks):
-        @pl.when(n != task)
-        def _():
-            back_from(gi_own, gi_in, gi_ss, gi_rs, n).wait_recv()
-            back_from(out_own, out_in, out_ss, out_rs, n).wait_recv()
-
-    keep_gi.wait()
-    keep_out.wait()
+    strip_rows = gw_full.shape[1]
+    for q in range(tasks):
+        for s in range(2):
+            gw_done[pl.ds((s * tasks + q) * strip_rows, strip_rows), :] = gw_full[2 * q + s].astype(F32)
+    keep_gw = pltpu.make_async_copy(gw_done, gw_ref, keep_sem.at[2 * members])
+    keep_gw.start()
+    for keep in (*keep_gi, *keep_out, keep_gw):
+        keep.wait()
 
     w_across.wait_send()
 
@@ -473,34 +489,21 @@
             back_copy(out_own, out_in, out_ss, out_rs, n).wait_send()
 
 
-def lay_out(block, out_hbm, gi_hbm, gw_hbm, out_ref, gi_ref, gw_ref, out_in, gi_in, gw_in, out_done, gi_done, gw_done, sems, done_sems):
-    tasks, padded, channels = out_hbm.shape
-    members, _, rows, _ = out_ref.shape
-    loads = []
-    for i, (source, into) in enumerate(((gi_hbm, gi_in), (out_hbm, out_in))):
-        for m in range(members):
-            part = pl.ds(m * rows, rows)
-            loads.append(pltpu.make_async_copy(source.at[part], into.at[part], sems.at[i * members + m]))
-    loads.append(pltpu.make_async_copy(gw_hbm, gw_in, sems.at[2 * members]))
+def hand_over(out_from, gi_from, gw_from, out_ref, gi_ref, gw_ref, out_here, gi_here, gw_here, in_sems, out_sems):
+    members, block, _, _ = out_ref.shape
+    half = block // 2
+    size = gw_ref.shape[0] // 4
+    moves = []
+    for source, here, ref in ((gi_from, gi_here, gi_ref), (out_from, out_here, out_ref)):
+        moves += [(source, here, ref, (m, pl.ds(i * half, half))) for m in range(members) for i in range(2)]
+    moves += [(gw_from, gw_here, gw_ref, (pl.ds(i * size, size),)) for i in range(4)]
+    loads = [pltpu.make_async_copy(a.at[w], h.at[w], in_sems.at[i]) for i, (a, h, _, w) in enumerate(moves)]
+    stores = [pltpu.make_async_copy(h.at[w], r.at[w], out_sems.at[i]) for i, (_, h, r, w) in enumerate(moves)]
     for load in loads:
         load.start()
-    to_places = gather_back(block, padded, rows)
-    stores = []
-    for i, (into, ready, ref) in enumerate(((gi_in, gi_done, gi_ref), (out_in, out_done, out_ref))):
-        for m in range(members):
-            loads[i * members + m].wait()
-            flat = into[pl.ds(m * rows, rows)].reshape(rows * padded, channels)
-            moved = jnp.dot(to_places, flat, preferred_element_type=F32).astype(BF)
-            ready[m] = moved.reshape(block, rows, channels)
-            stores.append(pltpu.make_async_copy(ready.at[m], ref.at[m], done_sems.at[i * members + m]))
-            stores[-1].start()
-    loads[-1].wait()
-    strip_rows = gw_in.shape[1]
-    for q in range(tasks):
-        for s in range(2):
-            gw_done[pl.ds((s * tasks + q) * strip_rows, strip_rows), :] = gw_in[2 * q + s].astype(F32)
-    stores.append(pltpu.make_async_copy(gw_done, gw_ref, done_sems.at[2 * members]))
-    stores[-1].start()
+    for load, store in zip(loads, stores):
+        load.wait()
+        store.start()
     for store in stores:
         store.wait()
 
@@ -526,7 +529,8 @@
     scratch = [
         vmem(features.shape, BF), vmem(features.shape, BF), field, field, ext, ext, strip, strip, strip, strip, ext, ext, wide, wide,
         vmem((groups, 2, piece, channels), BF),
-        field, field,
+        field, field, field, field,
+        vmem(features.shape, BF), vmem(features.shape, BF), vmem(weight.shape, F32),
         vmem((2, 2, piece, tasks * padded), BF),
         vmem((lines, 2, piece, channels), F32),
         vmem((lines, 2, piece, channels), BF),
@@ -542,35 +546,33 @@
         dma((2 * lines,)), dma((groups,)), dma((groups,)), dma((groups,)),
         dma((tasks,)), dma((tasks,)), dma((tasks,)), dma((tasks,)),
         dma((lines,)), dma((lines,)), dma((3, 2)), dma((2,)), dma((2, 2)),
-        dma((2 * tasks,)), dma((2, tasks)), dma((tasks,)), dma((count,)), dma((tasks,)), dma((2,)), dma((4,)),
+        dma((2 * tasks,)), dma((2, tasks)), dma((tasks,)), dma((count,)), dma((tasks,)), dma((2 * members + 1,)), dma((4,)),
     ]
-    whole = pl.BlockSpec(memory_space=pltpu.VMEM)
     scalar = pl.BlockSpec(memory_space=pltpu.SMEM)
     any_place = pl.BlockSpec(memory_space=pl.ANY)
-    back = jax.ShapeDtypeStruct((tasks, padded, channels), BF)
+    results = (
+        jax.ShapeDtypeStruct(features.shape, BF),
+        jax.ShapeDtypeStruct(features.shape, BF),
+        jax.ShapeDtypeStruct(weight.shape, F32),
+    )
     parts = pl.pallas_call(
         functools.partial(kernel, count, groups),
-        out_shape=(back, back, jax.ShapeDtypeStruct((count, strip_rows, channels), BF)),
+        out_shape=results,
         in_specs=[any_place, any_place, any_place, scalar, scalar],
-        out_specs=(any_place, any_place, whole),
+        out_specs=(any_place,) * 3,
         scratch_shapes=scratch,
         compiler_params=pltpu.CompilerParams(
             collective_id=0, has_side_effects=True, vmem_limit_bytes=60 * 1024 * 1024
         ),
     )(features, grad_out, weight, band_width, band_start)
     output, grad_input, grad_weight = pl.pallas_call(
-        functools.partial(lay_out, block),
-        out_shape=(
-            jax.ShapeDtypeStruct(features.shape, BF),
-            jax.ShapeDtypeStruct(features.shape, BF),
-            jax.ShapeDtypeStruct(weight.shape, F32),
-        ),
+        hand_over,
+        out_shape=results,
         in_specs=[any_place] * 3,
         out_specs=(any_place,) * 3,
         scratch_shapes=[
-            field, field, vmem((count, strip_rows, channels), BF),
             vmem(features.shape, BF), vmem(features.shape, BF), vmem(weight.shape, F32),
-            dma((2 * members + 1,)), dma((2 * members + 1,)),
+            dma((4 * members + 4,)), dma((4 * members + 4,)),
         ],
         compiler_params=pltpu.CompilerParams(vmem_limit_bytes=60 * 1024 * 1024),
     )(*parts)

time: 67.6 us -> 64.3 us (0.951)
  Pallas kernels: 66.8 us -> 63.5 us
    pallas_call x2, Pallas kernels: 66.8 us -> 63.5 us  [the longest x1 61 us: on_device(): pl.pallas_call(functools.partial(kernel, count, groups), out_shape=result...]
where the time goes in v4:
time: 64.3 us; the launch traced here: 64.1 us
  Pallas kernels  63.5 us (99%)
    pallas_call x1, Pallas kernels, on_device(): pl.pallas_call(functools.partial(kernel, count, groups), out_shape=result...  61 us
    pallas_call x1, Pallas kernels, on_device(): pl.pallas_call(hand_over, out_shape=results, in_specs=[any_place] * 3, ou...  2.5 us

profile of v4, /device:TPU:1, one launch (start us, length us, event | category | flops | bytes accessed | tf_op | source)
XLA Modules:
  0.0 64.1 jit_solution(6635143157611101456)
XLA Ops:
  0.6 61.0 %shard_map.76 = (bf16[2,90,4,512]{3,2,1,0:T(4,128)(2,1)}, bf16[2,90,4,512]{3,2,1,0:T(4,128)(2,1)}, f32[256,512]{1,0:T(8,128)}) custom-call(bf16[2,90,4,512]{3,2,1,0:T(4,128)(2,1)} %bitcast.4, bf16[2,90,4,512]{3,2,1,0:T(4,128)(2,1)} %bitcast.5, bf16[256,512]{1,0:T(8,128)(2,1)} %w_hbm.1, s32[4]{0:T(128)} %width_ref.1, s32[4]{0:T(128)} %start_ref.1), custom_call_target="tpu_custom_call" | custom-call | tf_op jit(solution)/shard_map/pallas_call | solution.py:558
  61.6 2.5 %shard_map.77 = (bf16[2,90,4,512]{3,2,1,0:T(4,128)(2,1)}, bf16[2,90,4,512]{3,2,1,0:T(4,128)(2,1)}, f32[256,512]{1,0:T(8,128)}) custom-call(bf16[2,90,4,512]{3,2,1,0:T(4,128)(2,1)} %get-tuple-element.9.out_from, bf16[2,90,4,512]{3,2,1,0:T(4,128)(2,1)} %get-tuple-element.10.gi_from, f32[256,512]{1,0:T(8,128)} %get-tuple-element.11.gw_from), custom_call_target="tpu_custom_call" | custom-call | tf_op jit(solution)/shard_map/pallas_call | solution.py:568

commit v5 on v4

--- a/solution.py
+++ b/solution.py
@@ -77,10 +77,10 @@
     out_ref, gi_ref, gw_ref,
     f_ref, g_ref, f_send, g_send, f_ext, g_ext, f_plus, f_minus, g_plus, g_minus, sums, differences, resp, adj, w_all,
     out_own, gi_own, out_in, gi_in, out_done, gi_done, gw_done,
-    turned, gw_own, gw_half, gw_mate, gw_sum, gw_hop, gw_line, gw_part, gw_part_in, gw_full,
+    turned, gw_own, gw_half, gw_mate, gw_sum, gw_hop, gw_line, gw_cross, gw_part, gw_part_in, gw_full,
     f_ss, f_rs, f_fs, g_ss, g_rs, g_fs, w_ss, w_rs, w_ms, w_mr,
     out_ss, out_rs, gi_ss, gi_rs,
-    a_ss, a_rs, b_ss, b_hs, b_rs, c_ss, c_rs, d_ss, d_rs, d_ms, keep_sem, load_sem,
+    a_ss, a_rs, b_ss, b_hs, b_rs, x_ss, x_rs, c_ss, c_rs, d_ss, d_rs, d_ms, keep_sem, load_sem,
 ):
     members, block, rows, channels = f_hbm.shape
     padded = f_send.shape[1]
@@ -140,6 +140,8 @@
     def w_second(o):
         return remote(w_all.at[across, half], w_all.at[across, half], w_ss.at[lines + o], w_rs.at[across], lon, along(o))
 
+    far_first = sorted(range(1, tasks), key=lambda o: (min(o, tasks - o) < tasks // 2, o % 2 == 0, abs(o - tasks // 2)))
+
     def w_from(other):
         return remote(w_all.at[other, half], w_all.at[other, half], w_ss.at[0], w_rs.at[other], lon, other)
 
@@ -159,8 +161,7 @@
         slot = 2 * lax.rem(task + tasks - o, tasks) + 1 - half
         return remote(ext.at[slot], ext.at[slot], fs.at[o], rs.at[slot], mate, ens)
 
-    @pl.loop(1, tasks)
-    def _(o):
+    for o in far_first:
         in_copy(g_send, g_ext, g_ss, g_rs, o).start()
 
     w_across.start()
@@ -183,22 +184,19 @@
     row = lax.rem(task, rows)
     fill_strips(g_plus, g_minus, width_ref[row], start_ref[row], block, padded, count, True)
 
-    @pl.loop(1, tasks)
-    def _(o):
+    for o in far_first:
         in_copy(g_send, g_ext, g_ss, g_rs, o).wait_send()
         in_copy(f_send, f_ext, f_ss, f_rs, o).start()
 
     fill_strips(f_plus, f_minus, width_ref[row], start_ref[row], block, padded, count, False)
 
     def pass_on(ext, ss, fs, rs):
-        @pl.loop(1, tasks)
-        def _(o):
+        for o in far_first:
             in_from(ext, ss, rs, o).wait_recv()
             forward(ext, fs, rs, o).start()
 
     def complete(ext, fs, rs):
-        @pl.loop(0, tasks)
-        def _(o):
+        for o in (0, *far_first):
             forwarded(ext, fs, rs, o).wait_recv()
 
         @pl.loop(0, tasks)
@@ -212,8 +210,8 @@
             differences[b] = apart.astype(BF)
             differences[tasks + b] = (-apart).astype(BF)
 
-    def convolve(plus, minus, result):
-        @pl.loop(0, tasks // 2)
+    def convolve(plus, minus, result, which):
+        @pl.loop(which * (tasks // 4), (which + 1) * (tasks // 4))
         def _(n):
             window = pl.ds(2 * n + half, tasks)
             both = jnp.dot(plus[...], sums[window].reshape(tasks * padded, channels), preferred_element_type=F32)
@@ -245,8 +243,10 @@
 
     def send_back(own, into, ss, rs, c):
         chunk = tasks // 2
-        for n in range(c * chunk, (c + 1) * chunk):
-            @pl.when(n != task)
+        for o in far_first:
+            n = lax.rem(task + o, tasks)
+
+            @pl.when(lax.div(n, chunk) == c)
             def _():
                 back_copy(own, into, ss, rs, n).start()
 
@@ -265,7 +265,8 @@
         w_mate(along(o)).start()
 
     w_mate(across).start()
-    convolve(g_plus, g_minus, adj)
+    convolve(g_plus, g_minus, adj, 0)
+    convolve(g_plus, g_minus, adj, 1)
 
     @pl.loop(1, lines)
     def _(o):
@@ -276,7 +277,8 @@
     def _(o):
         w_mate_from(lax.rem(ens + o, groups)).wait_recv()
 
-    for c in range(2):
+    first_half = 1 - lax.div(task, tasks // 2)
+    for c in (first_half, 1 - first_half):
         mix(adj, gi_own, c, True)
         send_back(gi_own, gi_in, gi_ss, gi_rs, c)
 
@@ -301,75 +303,97 @@
     ahead = lax.rem(line + 1, lines)
     back = lax.rem(line + lines - 1, lines)
     opposite = lax.rem(line + 2, lines)
-    ways = ((0, ahead, back), (1, back, ahead))
-
-    def chip_sum(to, i):
-        return gw_own[to, i] + gw_mate[to, i].astype(F32)
-
-    def hop(i):
-        _, to, _ = ways[i]
-        return remote(gw_sum.at[opposite, i], gw_hop.at[i], b_ss.at[0, i], b_hs.at[i], lon, 2 * to + side)
-
-    def plain(i):
-        _, to, _ = ways[i]
-        return remote(gw_sum.at[to, 1 - i], gw_line.at[i, 1 - i], b_ss.at[1, i], b_rs.at[i, 1 - i], lon, 2 * to + side)
-
-    def added(i):
-        _, to, _ = ways[i]
-        return remote(gw_sum.at[to, i], gw_line.at[i, i], b_ss.at[2, i], b_rs.at[i, i], lon, 2 * to + side)
+    ways = ((0, ahead), (1, back))
+    sides = (1 - side, side)
+    rows_half = piece // 2
+
+    def part(i):
+        return pl.ds(i * rows_half, rows_half)
+
+    def chip_sum(to, s, i):
+        return gw_own[to, s, part(i)] + gw_mate[to, s, part(i)].astype(F32)
+
+    def hop(t, i):
+        return remote(gw_sum.at[opposite, sides[t], part(i)], gw_hop.at[t, i], b_ss.at[0, t, i], b_hs.at[t, i],
+                      lon, 2 * ways[i][1] + side)
+
+    def plain(t, i):
+        return remote(gw_sum.at[ways[i][1], sides[t], part(1 - i)], gw_line.at[t, i, 1 - i], b_ss.at[1, t, i], b_rs.at[t, i, 1 - i],
+                      lon, 2 * ways[i][1] + side)
+
+    def added(t, i):
+        return remote(gw_sum.at[ways[i][1], sides[t], part(i)], gw_line.at[t, i, i], b_ss.at[2, t, i], b_rs.at[t, i, i],
+                      lon, 2 * ways[i][1] + side)
+
+    def start_hop(t):
+        for i in range(2):
+            gw_sum[opposite, sides[t], part(i)] = chip_sum(opposite, sides[t], i).astype(BF)
+            hop(t, i).start()
+
+    def start_plain(t):
+        for i, to in ways:
+            gw_sum[to, sides[t], part(1 - i)] = chip_sum(to, sides[t], 1 - i).astype(BF)
+            plain(t, i).start()
+
+    def start_added(t):
+        for i, to in ways:
+            hop(t, i).wait_recv()
+            gw_sum[to, sides[t], part(i)] = (chip_sum(to, sides[t], i) + gw_hop[t, i].astype(F32)).astype(BF)
+            added(t, i).start()
+
+    def line_sum(t):
+        for i in range(2):
+            plain(t, i).wait_recv()
+            added(t, i).wait_recv()
+        total = gw_own[line, sides[t]] + gw_mate[line, sides[t]].astype(F32)
+        return total + (gw_line[t, 0].astype(F32) + gw_line[t, 1].astype(F32)).reshape(piece, channels)
 
     a_copy(opposite).wait_recv()
-    for i in range(2):
-        gw_sum[opposite, i] = chip_sum(opposite, i).astype(BF)
-        hop(i).start()
+    start_hop(0)
     for to in order[2:]:
         gw_half[to] = terms(to, 1 - half).astype(BF)
         a_copy(to).start()
     for to in order[1:]:
         gw_own[to] = terms(to, half)
-    for i, to, _ in ways:
+    for _, to in ways:
         a_copy(to).wait_recv()
-        gw_sum[to, 1 - i] = chip_sum(to, 1 - i).astype(BF)
-        plain(i).start()
+    start_plain(0)
+    start_hop(1)
     a_copy(line).wait_recv()
 
     complete(f_ext, f_fs, f_rs)
-    convolve(f_plus, f_minus, resp)
-
-    for i, to, _ in ways:
-        hop(i).wait_recv()
-        gw_sum[to, i] = (chip_sum(to, i) + gw_hop[i].astype(F32)).astype(BF)
-        added(i).start()
-
-    mix(resp, out_own, 0, False)
-    send_back(out_own, out_in, out_ss, out_rs, 0)
-    mix(resp, out_own, 1, False)
-
-    for i in range(2):
-        plain(i).wait_recv()
-        added(i).wait_recv()
-    for s in range(2):
-        total = chip_sum(line, s) + gw_line[0, s].astype(F32) + gw_line[1, s].astype(F32)
-        gw_part[s] = total.astype(BF).reshape(gw_part.shape[1:])
-
-    def c_place(o):
-        s = lax.rem(side + lax.div(o, tasks), 2)
-        return s, lax.rem(task + lax.rem(o, tasks), tasks)
+    convolve(f_plus, f_minus, resp, 0)
+    start_added(0)
+    start_plain(1)
+    convolve(f_plus, f_minus, resp, 1)
+    start_added(1)
+
+    own_half = lax.div(task, tasks // 2)
+    mix(resp, out_own, 1 - own_half, False)
+    send_back(out_own, out_in, out_ss, out_rs, 1 - own_half)
+
+    cross = remote(gw_cross.at[0], gw_cross.at[1], x_ss, x_rs, beside, across)
+    gw_cross[0] = line_sum(0).astype(BF)
+    cross.start()
+    mix(resp, out_own, own_half, False)
+
+    total = line_sum(1)
+    cross.wait_recv()
+    gw_part[...] = (total + gw_cross[1].astype(F32)).astype(BF).reshape(gw_part.shape)
 
     def c_copy(o):
-        s, q = c_place(o)
-        return remote(gw_part.at[s, q], gw_part_in.at[side, task], c_ss.at[o], c_rs.at[side, task], 2 * q + half, 2 * line + s)
+        q = lax.rem(task + o, tasks)
+        return remote(gw_part.at[q], gw_part_in.at[task], c_ss.at[o], c_rs.at[task], 2 * q + half, ens)
 
     def c_from(o):
-        s, q = c_place(o)
-        return remote(gw_part.at[s, q], gw_part_in.at[s, q], c_ss.at[o], c_rs.at[s, q], 2 * q + half, 2 * line + s)
-
-    @pl.loop(1, 2 * tasks)
-    def _(o):
+        q = lax.rem(task + o, tasks)
+        return remote(gw_part.at[q], gw_part_in.at[q], c_ss.at[o], c_rs.at[q], 2 * q + half, ens)
+
+    for o in far_first:
         c_copy(o).start()
 
-    send_back(out_own, out_in, out_ss, out_rs, 1)
-    gw_part_in[side, task] = gw_part[side, task]
+    send_back(out_own, out_in, out_ss, out_rs, own_half)
+    gw_part_in[task] = gw_part[task]
 
     def d_copy(o):
         return remote(gw_full.at[lon], gw_full.at[lon], d_ss.at[o], d_rs.at[lon], 2 * lax.rem(task + o, tasks) + half, ens)
@@ -404,19 +428,16 @@
     to_places = gather_back(block, padded, rows)
     keep_gi = finish(gi_ref, gi_done, gi_own, gi_in, gi_ss, gi_rs, 0)
 
-    @pl.loop(1, 2 * tasks)
-    def _(o):
+    for o in far_first:
         c_from(o).wait_recv()
 
     total = None
-    for e in range(2):
-        for q in range(tasks):
-            term = gw_part_in[e, q].astype(F32)
-            total = term if total is None else total + term
+    for q in range(tasks):
+        term = gw_part_in[q].astype(F32)
+        total = term if total is None else total + term
     gw_full[lon] = total.astype(BF)
 
-    @pl.loop(1, tasks)
-    def _(o):
+    for o in far_first:
         d_copy(o).start()
 
     d_mate(0).start()
@@ -456,12 +477,14 @@
     def _(o):
         a_copy(o).wait_send()
 
-    for i in range(2):
-        hop(i).wait_send()
-        plain(i).wait_send()
-        added(i).wait_send()
-
-    @pl.loop(1, 2 * tasks)
+    for t in range(2):
+        for i in range(2):
+            hop(t, i).wait_send()
+            plain(t, i).wait_send()
+            added(t, i).wait_send()
+    cross.wait_send()
+
+    @pl.loop(1, tasks)
     def _(o):
         c_copy(o).wait_send()
 
@@ -536,17 +559,18 @@
         vmem((lines, 2, piece, channels), BF),
         vmem((lines, 2, piece, channels), BF),
         vmem((lines, 2, piece, channels), BF),
+        vmem((2, 2, piece // 2, channels), BF),
+        vmem((2, 2, 2, piece // 2, channels), BF),
         vmem((2, piece, channels), BF),
-        vmem((2, 2, piece, channels), BF),
-        vmem((2, tasks, strip_rows, channels), BF),
-        vmem((2, tasks, strip_rows, channels), BF),
+        vmem((tasks, strip_rows, channels), BF),
+        vmem((tasks, strip_rows, channels), BF),
         vmem((count, strip_rows, channels), BF),
         dma((tasks,)), dma((count,)), dma((tasks,)),
         dma((tasks,)), dma((count,)), dma((tasks,)),
         dma((2 * lines,)), dma((groups,)), dma((groups,)), dma((groups,)),
         dma((tasks,)), dma((tasks,)), dma((tasks,)), dma((tasks,)),
-        dma((lines,)), dma((lines,)), dma((3, 2)), dma((2,)), dma((2, 2)),
-        dma((2 * tasks,)), dma((2, tasks)), dma((tasks,)), dma((count,)), dma((tasks,)), dma((2 * members + 1,)), dma((4,)),
+        dma((lines,)), dma((lines,)), dma((3, 2, 2)), dma((2, 2)), dma((2, 2, 2)), dma(()), dma(()),
+        dma((tasks,)), dma((tasks,)), dma((tasks,)), dma((count,)), dma((tasks,)), dma((2 * members + 1,)), dma((4,)),
     ]
     scalar = pl.BlockSpec(memory_space=pltpu.SMEM)
     any_place = pl.BlockSpec(memory_space=pl.ANY)

time: 64.3 us -> 63.5 us (0.988)
  Pallas kernels: 63.5 us -> 62.7 us
    pallas_call x1, Pallas kernels: 61 us -> 60.2 us  [on_device(): pl.pallas_call(functools.partial(kernel, count, groups), out_shape=result...]
where the time goes in v5:
time: 63.5 us; the launch traced here: 63.3 us
  Pallas kernels  62.7 us (99%)
  between operations  0.64 us (1%)
    pallas_call x1, Pallas kernels, on_device(): pl.pallas_call(functools.partial(kernel, count, groups), out_shape=result...  60.2 us
    pallas_call x1, Pallas kernels, on_device(): pl.pallas_call(hand_over, out_shape=results, in_specs=[any_place] * 3, ou...  2.5 us

profile of v5, /device:TPU:1, one launch (start us, length us, event | category | flops | bytes accessed | tf_op | source)
XLA Modules:
  0.0 63.3 jit_solution(10692002420848032150)
XLA Ops:
  0.6 60.2 %shard_map.76 = (bf16[2,90,4,512]{3,2,1,0:T(4,128)(2,1)}, bf16[2,90,4,512]{3,2,1,0:T(4,128)(2,1)}, f32[256,512]{1,0:T(8,128)}) custom-call(bf16[2,90,4,512]{3,2,1,0:T(4,128)(2,1)} %bitcast.4, bf16[2,90,4,512]{3,2,1,0:T(4,128)(2,1)} %bitcast.5, bf16[256,512]{1,0:T(8,128)(2,1)} %w_hbm.1, s32[4]{0:T(128)} %width_ref.1, s32[4]{0:T(128)} %start_ref.1), custom_call_target="tpu_custom_call" | custom-call | tf_op jit(solution)/shard_map/pallas_call | solution.py:582
  60.8 2.5 %shard_map.77 = (bf16[2,90,4,512]{3,2,1,0:T(4,128)(2,1)}, bf16[2,90,4,512]{3,2,1,0:T(4,128)(2,1)}, f32[256,512]{1,0:T(8,128)}) custom-call(bf16[2,90,4,512]{3,2,1,0:T(4,128)(2,1)} %get-tuple-element.9.out_from, bf16[2,90,4,512]{3,2,1,0:T(4,128)(2,1)} %get-tuple-element.10.gi_from, f32[256,512]{1,0:T(8,128)} %get-tuple-element.11.gw_from), custom_call_target="tpu_custom_call" | custom-call | tf_op jit(solution)/shard_map/pallas_call | solution.py:592

commit v6 on v5

--- a/solution.py
+++ b/solution.py
@@ -108,24 +108,25 @@
         greet(lon, 2 * lax.rem(line + o, lines) + side)
     greet(beside, across)
 
+    def stage_member(ref, buffer, m):
+        flat = ref[m].reshape(block * rows, channels)
+        moved = jnp.dot(to_rows, flat, preferred_element_type=F32).astype(BF)
+        buffer[pl.ds(m * rows, rows)] = moved.reshape(rows, padded, channels)
+
     def stage(ref, buffer, ext):
         for m in range(members):
-            flat = ref[m].reshape(block * rows, channels)
-            moved = jnp.dot(to_rows, flat, preferred_element_type=F32).astype(BF)
-            buffer[pl.ds(m * rows, rows)] = moved.reshape(rows, padded, channels)
+            stage_member(ref, buffer, m)
         ext[lon] = buffer[task]
 
     piece = w_all.shape[2]
-    load_g = pltpu.make_async_copy(g_hbm, g_ref, load_sem.at[0])
+    load_g = [pltpu.make_async_copy(g_hbm.at[m], g_ref.at[m], load_sem.at[4 + m]) for m in range(members)]
     load_w = [pltpu.make_async_copy(w_hbm.at[pl.ds(i * piece, piece)], w_all.at[ens, i], load_sem.at[1 + i]) for i in range(2)]
     load_f = pltpu.make_async_copy(f_hbm, f_ref, load_sem.at[3])
-    for load in (load_g, *load_w, load_f):
+    for load in (*load_g, *load_w, load_f):
         load.start()
     to_rows = spread(block, padded, rows)
-    load_g.wait()
-    stage(g_ref, g_send, g_ext)
-    for load in load_w:
-        load.wait()
+    load_g[0].wait()
+    stage_member(g_ref, g_send, 0)
 
     pl.semaphore_wait(barrier, tasks + lines)
 
@@ -161,8 +162,17 @@
         slot = 2 * lax.rem(task + tasks - o, tasks) + 1 - half
         return remote(ext.at[slot], ext.at[slot], fs.at[o], rs.at[slot], mate, ens)
 
-    for o in far_first:
-        in_copy(g_send, g_ext, g_ss, g_rs, o).start()
+    for m in range(members):
+        if m:
+            load_g[m].wait()
+            stage_member(g_ref, g_send, m)
+        for o in far_first:
+            @pl.when(lax.div(lax.rem(task + o, tasks), rows) == m)
+            def _():
+                in_copy(g_send, g_ext, g_ss, g_rs, o).start()
+    g_ext[lon] = g_send[task]
+    for load in load_w:
+        load.wait()
 
     w_across.start()
 
@@ -570,7 +580,7 @@
         dma((2 * lines,)), dma((groups,)), dma((groups,)), dma((groups,)),
         dma((tasks,)), dma((tasks,)), dma((tasks,)), dma((tasks,)),
         dma((lines,)), dma((lines,)), dma((3, 2, 2)), dma((2, 2)), dma((2, 2, 2)), dma(()), dma(()),
-        dma((tasks,)), dma((tasks,)), dma((tasks,)), dma((count,)), dma((tasks,)), dma((2 * members + 1,)), dma((4,)),
+        dma((tasks,)), dma((tasks,)), dma((tasks,)), dma((count,)), dma((tasks,)), dma((2 * members + 1,)), dma((4 + members,)),
     ]
     scalar = pl.BlockSpec(memory_space=pltpu.SMEM)
     any_place = pl.BlockSpec(memory_space=pl.ANY)

time: 63.5 us -> 66 us (1.039)
  Pallas kernels: 62.7 us -> 65.1 us
    pallas_call x1, Pallas kernels: 60.2 us -> 62.6 us  [on_device(): pl.pallas_call(functools.partial(kernel, count, groups), out_shape=result...]
where the time goes in v6:
time: 66 us; the launch traced here: 65.7 us
  Pallas kernels  65.1 us (99%)
    pallas_call x1, Pallas kernels, on_device(): pl.pallas_call(functools.partial(kernel, count, groups), out_shape=result...  62.6 us
    pallas_call x1, Pallas kernels, on_device(): pl.pallas_call(hand_over, out_shape=results, in_specs=[any_place] * 3, ou...  2.5 us

profile of v6, /device:TPU:1, one launch (start us, length us, event | category | flops | bytes accessed | tf_op | source)
XLA Modules:
  0.0 65.7 jit_solution(710663674804932945)
XLA Ops:
  0.6 62.6 %shard_map.76 = (bf16[2,90,4,512]{3,2,1,0:T(4,128)(2,1)}, bf16[2,90,4,512]{3,2,1,0:T(4,128)(2,1)}, f32[256,512]{1,0:T(8,128)}) custom-call(bf16[2,90,4,512]{3,2,1,0:T(4,128)(2,1)} %bitcast.4, bf16[2,90,4,512]{3,2,1,0:T(4,128)(2,1)} %bitcast.5, bf16[256,512]{1,0:T(8,128)(2,1)} %w_hbm.1, s32[4]{0:T(128)} %width_ref.1, s32[4]{0:T(128)} %start_ref.1), custom_call_target="tpu_custom_call" | custom-call | tf_op jit(solution)/shard_map/pallas_call | solution.py:592
  63.2 2.5 %shard_map.77 = (bf16[2,90,4,512]{3,2,1,0:T(4,128)(2,1)}, bf16[2,90,4,512]{3,2,1,0:T(4,128)(2,1)}, f32[256,512]{1,0:T(8,128)}) custom-call(bf16[2,90,4,512]{3,2,1,0:T(4,128)(2,1)} %get-tuple-element.9.out_from, bf16[2,90,4,512]{3,2,1,0:T(4,128)(2,1)} %get-tuple-element.10.gi_from, f32[256,512]{1,0:T(8,128)} %get-tuple-element.11.gw_from), custom_call_target="tpu_custom_call" | custom-call | tf_op jit(solution)/shard_map/pallas_call | solution.py:602
